TPU v7x, 256 devices: a whole 4x4x8 slice. The times are simulated.
256 devices in a mesh: frame: 16 (over y_lo, x, core), seq: 16 (over y_hi, z).
Axes of the slice: x: 4, y: 4 (y_hi: 2, y_lo: 2; y = y_hi * 2 + y_lo), z: 8, core: 2. Of those that a mesh axis runs over, the one named last changes fastest.
Arguments:
- queue_tokens: bfloat16 [16, 640, 3072], P('frame', 'seq'), may hold values from -6 to 6
- timesteps: int32 [16], P('frame'), may hold values from 0 to 991, as said below
- fresh_noise: bfloat16 [640, 3072], P('seq'), may hold values from -6 to 6
- w_mod: bfloat16 [512, 9216], P(None, 'seq'), may hold values from -0.25 to 0.25
- w_qkv: bfloat16 [3072, 3, 2048], P(None, None, 'seq'), may hold values from -0.109375 to 0.109375
- q_gain: float32 [64], replicated, may hold values from 0.9 to 6
- k_gain: float32 [64], replicated, may hold values from 0.9 to 6
- w_out: bfloat16 [2048, 3072], P('seq'), may hold values from -0.75 to 0.75
Outputs:
- queue_next: bfloat16 [16, 640, 3072], P('frame', 'seq')
Inputs may be any that keep to these rules, and one draw needn't show every extreme that they name: `timesteps`: slot number s has a level from s * 62 to (s + 1) * 62 - 1, so levels rise strictly along the queue; the first slot has level 0 and the last slot level 991.
All inputs are finite; a program needn't handle non-finite values.
Results may differ from a plain program's by a relative error of at most 0.03.
The roundings to bfloat16 on the way count: a program that leaves them out, or rounds other values in their place, can miss the bound.
Values may be sent and summed in bfloat16 or wider, within the bound.
A program may use at most 64 MiB of HBM per device.

v0:
```python
import math

import jax
import jax.numpy as jnp
from jax import lax
from jax.sharding import PartitionSpec as P

TEMB = 512


def shifted(value, axis, by):
    peers = lax.axis_size(axis)
    pairs = [(i, i + by) for i in range(peers) if 0 <= i + by < peers]
    return lax.ppermute(value, axis, pairs)


def embed_steps(levels):
    halfway = TEMB // 2
    frequency = jnp.exp(-math.log(10000.0) * jnp.arange(halfway, dtype=jnp.float32) / halfway)
    angles = levels.astype(jnp.float32)[:, None] * frequency[None, :]
    return jnp.concatenate([jnp.cos(angles), jnp.sin(angles)], axis=-1)


def head_norm(values, gains):
    average = jnp.mean(values, axis=-1, keepdims=True)
    centred = values - average
    spread = jnp.mean(centred * centred, axis=-1, keepdims=True)
    return centred * lax.rsqrt(spread + 1e-06) * gains


def modulate(tok_rows, shift_vec, scale_vec):
    widened = tok_rows.astype(jnp.float32)
    average = jnp.mean(widened, axis=-1, keepdims=True)
    centred = widened - average
    spread = jnp.mean(centred * centred, axis=-1, keepdims=True)
    normed = centred * lax.rsqrt(spread + 1e-05)
    return (normed * (1.0 + scale_vec) + shift_vec).astype(jnp.bfloat16)


def attend(queries, key_rows, value_rows):
    length = queries.shape[0]
    block_len = math.gcd(length, 512)
    head_count = queries.shape[1]
    head_size = queries.shape[2]
    blocks = queries.reshape(length // block_len, block_len, head_count, head_size)

    def one_block(query_block):
        scores = jnp.einsum(
            "qhc,fkhc->hqfk", query_block, key_rows, preferred_element_type=jnp.float32
        ) * head_size ** (-0.5)
        highest = jnp.max(scores, axis=(2, 3), keepdims=True)
        exponent = jnp.exp(scores - highest)
        summed = jnp.sum(exponent, axis=(2, 3), keepdims=True)
        weights = (exponent / summed).astype(jnp.bfloat16)
        mixed = jnp.einsum(
            "hqfk,fkhc->qhc", weights, value_rows, preferred_element_type=jnp.float32
        )
        return mixed.astype(jnp.bfloat16).reshape(block_len, head_count * head_size)

    return lax.map(one_block, blocks).reshape(length, head_count * head_size)


def body(queue_tokens, timesteps, fresh_noise, w_mod, w_qkv, q_gain, k_gain, w_out):
    frame_at = lax.axis_index("frame")
    frame_count = lax.axis_size("frame")
    width = queue_tokens.shape[2]
    tok_rows = queue_tokens[0]
    head_size = q_gain.shape[0]
    group_width = w_qkv.shape[2]
    local_heads = group_width // head_size
    condition = jax.nn.silu(embed_steps(timesteps)).astype(jnp.bfloat16)
    own_columns = jnp.dot(condition, w_mod, preferred_element_type=jnp.float32)
    modulation = lax.all_gather(own_columns, "seq", axis=1, tiled=True)
    shift_vec = modulation[0, :width]
    scale_vec = modulation[0, width : 2 * width]
    gate_vec = modulation[0, 2 * width :]
    modded = modulate(tok_rows, shift_vec, scale_vec)
    qkv_matrix = w_qkv.reshape(width, 3 * group_width)
    shard_rows = lax.all_gather(modded, "seq", axis=0, tiled=True)
    row_count = shard_rows.shape[0]
    joined = jnp.dot(shard_rows, qkv_matrix, preferred_element_type=jnp.float32)
    joined = joined.reshape(row_count, 3, local_heads, head_size)
    normed_q = head_norm(joined[:, 0], q_gain).astype(jnp.bfloat16)
    normed_k = head_norm(joined[:, 1], k_gain).astype(jnp.bfloat16)
    plain_v = joined[:, 2].astype(jnp.bfloat16)
    projected = jnp.concatenate([normed_q, normed_k, plain_v], axis=1).reshape(
        row_count, 3 * group_width
    )
    frame_len = projected.shape[0]
    queries = projected[:, :group_width].reshape(frame_len, local_heads, head_size)
    key_value = projected[:, group_width:][None]
    every_frame = lax.all_gather(key_value, "frame", axis=0, tiled=True)
    key_rows = every_frame[:, :, :group_width].reshape(
        frame_count, frame_len, local_heads, head_size
    )
    value_rows = every_frame[:, :, group_width:].reshape(
        frame_count, frame_len, local_heads, head_size
    )
    mixed = attend(queries, key_rows, value_rows)
    term = jnp.dot(mixed, w_out, preferred_element_type=jnp.float32)
    out_proj = lax.psum_scatter(
        lax.optimization_barrier(term.astype(jnp.bfloat16))
        .astype(jnp.float32)
        .astype(jnp.bfloat16),
        "seq",
        scatter_dimension=0,
        tiled=True,
    ).astype(jnp.float32)
    branch_term = gate_vec * out_proj
    updated = (tok_rows.astype(jnp.float32) + branch_term).astype(jnp.bfloat16)[None]
    arrived = shifted(updated, "frame", -1)
    return jnp.where(frame_at == frame_count - 1, fresh_noise[None], arrived)


def solution(mesh):
    return jax.shard_map(
        body,
        mesh=mesh,
        in_specs=(
            P("frame", "seq", None),
            P("frame"),
            P("seq", None),
            P(None, "seq"),
            P(None, None, "seq"),
            P(),
            P(),
            P("seq", None),
        ),
        out_specs=P("frame", "seq", None),
        check_vma=False,
    )
```

profile of v0, /device:TPU:1, one launch (start us, length us, event | category | flops | bytes accessed | tf_op | source)
XLA Modules:
  0.0 522.1 jit_solution(6290240060122247136)
XLA Ops:
  10.9 66.8 %all-reduce = f32[9216]{0:T(1024)S(1)} all-reduce(f32[9216]{0:T(1024)S(1)} %dynamic-update-slice), channel_id=2, replica_groups=mesh['frame'=16,'seq'=16] {'seq'}, use_global_device_ids=true, to_apply=%add | all-reduce | flops 9216 | bytes 73728
  82.0 2.8 copy.14
  84.8 100.7 %all-gather.5.cloned.1.call-done = bf16[640,3072]{1,0:T(8,128)(2,1)} async-done(((bf16[40,3072]{1,0:T(8,128)(2,1)}), bf16[640,3072]{1,0:T(8,128)(2,1)}) %all-gather.5.cloned.1.call-update) | async-done | bytes 3932176 | tf_op jit(solution)/shard_map/all_gather | solution.py:79
  185.5 4.2 fusion.9
  192.0 41.4 %all-gather.7.cloned.1.call-done = bf16[10240,256]{1,0:T(8,128)(2,1)} async-done(((bf16[640,256]{1,0:T(8,128)(2,1)}), bf16[10240,256]{1,0:T(8,128)(2,1)}) %all-gather.7.cloned.1.call-update) | async-done | bytes 5242896 | tf_op jit(solution)/shard_map/all_gather | solution.py:92
  233.4 4.5 fusion.25
  238.0 2.6 copy.16
  242.5 4.4 copy.17
  246.9 3.5 copy.20
  250.4 38.9 %while.10 = (s32[]{:T(128)}, bf16[5,128,128]{2,1,0:T(8,128)(2,1)}, bf16[5,128,2,64]{1,3,2,0:T(8,128)(2,1)}, bf16[16,640,2,64]{1,3,0,2:T(8,128)(2,1)S(1)}, bf16[16,640,2,64]{1,3,0,2:T(8,128)(2,1)}, /*index=5*/s32[]{:T(128)}) while((s32[]{:T(128)}, bf16[5,128,128]{2,1,0:T(8,128)(2,1)}, bf16[5,128,2,64]{1,3,2,0:T(8,128)(2,1)}, ...), condition=%wide.region_9.10_spmd, body=%wide.region_6.9_spmd.sunk | while | flops 694697472 | bytes 47388768 | solution.py:60
  250.4 2.4 multiply_reduce_fusion.4
  254.7 2.8 fusion.41
  258.2 2.4 multiply_reduce_fusion.4
  262.5 2.8 fusion.41
  266.0 2.4 multiply_reduce_fusion.4
  270.3 2.8 fusion.41
  273.8 2.4 multiply_reduce_fusion.4
  278.1 2.8 fusion.41
  281.6 2.4 multiply_reduce_fusion.4
  285.9 2.8 fusion.41
  289.4 4.0 convolution_convert_fusion
  293.4 208.4 %reduce-scatter.2.cloned.1.call-done = bf16[40,3072]{1,0:T(8,128)(2,1)} async-done(((bf16[640,3072]{1,0:T(8,128)(2,1)}), bf16[40,3072]{1,0:T(8,128)(2,1)}) %reduce-scatter.2.cloned.1.call-update) | async-done | bytes 245776 | tf_op jit(solution)/shard_map/reduce_scatter | solution.py:101
  502.9 7.0 %collective-permute-start = (bf16[1,40,3072]{2,1,0:T(8,128)(2,1)S(1)}, bf16[1,40,3072]{2,1,0:T(8,128)(2,1)S(1)}, u32[]{:S(2)}, u32[]{:S(2)}) collective-permute-start(bf16[1,40,3072]{2,1,0:T(8,128)(2,1)S(1)} %fusion.20), channel_id=1, source_target_pairs={{16,0},{32,16},{48,32},{64,48},{80,64},{96,80},{112,96},{128,112},... | collective-permute-start | bytes 737288 | tf_op jit(solution)/shard_map/ppermute | solution.py:14
  509.9 4.9 collective-permute-done
  (72 shorter events, 26.2 us)
Async XLA Ops:
  6.5 282.9 %copy-start = (bf16[128,3072]{1,0:T(8,128)(2,1)S(1)}, bf16[128,3072]{1,0:T(8,128)(2,1)}, u32[]{:S(2)}) copy-start(bf16[128,3072]{1,0:T(8,128)(2,1)} %param.17) | copy-start | bytes 2359300
  6.5 178.9 %all-gather.5.cloned.1.call-start = ((), (), s32[]{:S(2)}) async-start(), calls=%async_computation.1 | async-start | bytes 4177920 | tf_op jit(solution)/shard_map/all_gather | solution.py:79
  81.9 151.5 %all-gather.7.cloned.1.call-start = ((), (), s32[]{:S(2)}) async-start(), calls=%async_computation.3 | async-start | bytes 5570560 | tf_op jit(solution)/shard_map/all_gather | solution.py:92
  185.5 4.4 copy-start.4
  185.5 4.4 copy-start.5
  191.1 310.8 %reduce-scatter.2.cloned.1.call-start = ((), (), s32[]{:S(2)}) async-start(), calls=%async_computation.2 | async-start | bytes 4177920 | tf_op jit(solution)/shard_map/reduce_scatter | solution.py:101
  252.8 1.9 copy-start.2
  260.6 1.9 copy-start.2
  268.4 1.9 copy-start.2
  276.2 1.9 copy-start.2
  284.0 1.9 copy-start.2
  289.4 212.5 %copy-start.1 = (bf16[1,40,3072]{2,1,0:T(8,128)(2,1)S(1)}, bf16[1,40,3072]{2,1,0:T(8,128)(2,1)}, u32[]{:S(2)}) copy-start(bf16[1,40,3072]{2,1,0:T(8,128)(2,1)} %param.10) | copy-start | bytes 737284
  293.4 221.4 %copy-start.3 = (bf16[40,3072]{1,0:T(8,128)(2,1)S(1)}, bf16[40,3072]{1,0:T(8,128)(2,1)}, u32[]{:S(2)}) copy-start(bf16[40,3072]{1,0:T(8,128)(2,1)} %param.12) | copy-start | bytes 737284
  502.9 12.0 %collective-permute-start = (bf16[1,40,3072]{2,1,0:T(8,128)(2,1)S(1)}, bf16[1,40,3072]{2,1,0:T(8,128)(2,1)S(1)}, u32[]{:S(2)}, u32[]{:S(2)}) collective-permute-start(bf16[1,40,3072]{2,1,0:T(8,128)(2,1)S(1)} %fusion.20), channel_id=1, source_target_pairs={{16,0},{32,16},{48,32},{64,48},{80,64},{96,80},{112,96},{128,112},... | collective-permute-start | bytes 737288 | tf_op jit(solution)/shard_map/ppermute | solution.py:14
Sparse Core Ops, SparseCore 0:
  82.0 103.3 all-gather.4
  191.2 42.2 all-gather.6
  293.6 208.2 reduce-scatter.1
where the time goes:
time: 523 us; the launch traced here: 522 us
  waiting for transfers between devices  355 us (68%)
  blocking collectives  66.8 us (13%)
  matrix products  35.3 us (7%)
  local copies, waits for them, and re-layouts  27 us (5%)
  other arithmetic  15.6 us (3%)
  between operations  14.7 us (3%)
  starting transfers between devices  7.09 us (1%)
    reduce_scatter x1, waiting for transfers between devices, body(): lax.psum_scatter(lax.optimization_barrier(term.astype(jnp.bfloat16)).asty...  208 us
    all_gather x1, waiting for transfers between devices, body(): shard_rows = lax.all_gather(modded, 'seq', axis=0, tiled=True)  101 us
    unnamed x1, blocking collectives  66.8 us
    all_gather x1, waiting for transfers between devices, body(): every_frame = lax.all_gather(key_value, 'frame', axis=0, tiled=True)  41.4 us
    dot_general x5, matrix products, one_block(): jnp.einsum('hqfk,fkhc->qhc', weights, value_rows, preferred_element_type=...  13.8 us
    dot_general x5, matrix products, one_block(): jnp.einsum('qhc,fkhc->hqfk', query_block, key_rows, preferred_element_typ...  12 us
  transfers between devices with their start and end apart: 4, of which 4 were waited for; matrix products, arithmetic and copies ran while one was open for 1% of the time, Pallas kernels for 0%

commit v1 on v0

v1 whole, which is shorter than its diff:
```python
import math

import jax
import jax.numpy as jnp
from jax import lax
from jax.experimental import pallas as pl
from jax.experimental.pallas import tpu as pltpu
from jax.sharding import PartitionSpec as P

TEMB = 512
TOK = 40
D = 3072
GROUP = 128
HEAD = 64
BF = jnp.bfloat16
F32 = jnp.float32
MESH = pl.DeviceIdType.MESH
VMEM_LIMIT = 56 * 1024 * 1024


def embed_steps(levels):
    halfway = TEMB // 2
    frequency = jnp.exp(-math.log(10000.0) * jnp.arange(halfway, dtype=F32) / halfway)
    angles = levels.astype(F32)[:, None] * frequency[None, :]
    return jnp.concatenate([jnp.cos(angles), jnp.sin(angles)], axis=-1)


class Place:
    def __init__(self):
        f = lax.axis_index("frame")
        s = lax.axis_index("seq")
        self.f, self.s = f, s
        ylo, x, core = f // 8, (f // 2) % 4, f % 2
        yhi, z = s // 8, s % 8

        def frame(yl, xx, cc):
            return yl * 8 + xx * 2 + cc

        self.sib = (frame(ylo, x, 1 - core), s)
        self.ylo = (frame(1 - ylo, x, core), s)
        self.xp = (frame(ylo, (x + 1) % 4, core), s)
        self.xm = (frame(ylo, (x + 3) % 4, core), s)
        self.zp = (f, yhi * 8 + (z + 1) % 8)
        self.zm = (f, yhi * 8 + (z + 7) % 8)
        self.yhi = (f, (1 - yhi) * 8 + z)
        self.prev = ((f + 15) % 16, s)
        self.next = ((f + 1) % 16, s)
        self.at = frame
        self.coords = (ylo, x, core)

    def frame_at(self, dy, dx, dc):
        ylo, x, core = self.coords
        return self.at((ylo + dy) % 2, (x + dx) % 4, (core + dc) % 2)


class Link:
    def __init__(self, send_sem, recv_sem):
        self.send_sem, self.recv_sem = send_sem, recv_sem
        self.sent = []

    def _copy(self, i, src, dst, dev):
        return pltpu.make_async_remote_copy(
            src_ref=src,
            dst_ref=dst,
            send_sem=self.send_sem.at[i],
            recv_sem=self.recv_sem.at[i],
            device_id=dev,
            device_id_type=MESH,
        )

    def send(self, i, src, dst, dev):
        copy = self._copy(i, src, dst, dev)
        copy.start()
        self.sent.append(copy)

    def wait(self, i, dst, dev):
        self._copy(i, dst, dst, dev).wait_recv()

    def drain(self):
        for copy in self.sent:
            copy.wait_send()


def meet(devices):
    barrier = pltpu.get_barrier_semaphore()
    for dev in devices:
        pl.semaphore_signal(barrier, inc=1, device_id=dev, device_id_type=MESH)
    return lambda: pl.semaphore_wait(barrier, len(devices))


def to_block(rows):
    pieces = []
    for h in range(2):
        lo = rows[:, h * 1536 : h * 1536 + 768]
        hi = rows[:, h * 1536 + 768 : (h + 1) * 1536]
        pieces.append(jnp.concatenate([lo, hi], axis=0))
    return pieces


def head_norm_pair(x, gain, first):
    a = jnp.sum(jnp.where(first, x, 0.0), axis=-1, keepdims=True) * (1.0 / HEAD)
    b = jnp.sum(jnp.where(first, 0.0, x), axis=-1, keepdims=True) * (1.0 / HEAD)
    c = x - jnp.where(first, a, b)
    sq = c * c
    va = jnp.sum(jnp.where(first, sq, 0.0), axis=-1, keepdims=True) * (1.0 / HEAD)
    vb = jnp.sum(jnp.where(first, 0.0, sq), axis=-1, keepdims=True) * (1.0 / HEAD)
    return c * lax.rsqrt(jnp.where(first, va, vb) + 1e-06) * gain


def qkv_kernel(
    tok_ref, mod_ref, w_ref, wo_ref, qg_ref, kg_ref,
    q_out, kv_out, wop_out, gate_out,
    blocks, modbuf, modrows, modt, wp, wop, x_scr, swap_out, swap_in,
    send_sem, recv_sem,
):
    here = Place()
    f, s = here.f, here.s
    seq_peers = [(f, lax.rem(s + d, 16)) for d in range(1, 16)]
    ready = meet(seq_peers + [here.sib, here.ylo, here.xp, here.xm])
    link = Link(send_sem, recv_sem)

    tok = tok_ref[...].astype(F32)
    for h, piece in enumerate(to_block(tok)):
        blocks[0, h] = piece.astype(BF)
    modbuf[s] = mod_ref[...]
    ready()

    link.send(0, blocks.at[0], blocks.at[1], here.zp)
    link.send(1, blocks.at[0], blocks.at[2], here.zm)
    for d, dev in enumerate(seq_peers):
        link.send(10 + d, modbuf.at[s], modbuf.at[s], dev)

    def wo_part(i):
        rows = pl.ds(pl.multiple_of((i // 2) * 16, 16), 16)
        cols = pl.ds(pl.multiple_of((i % 2) * 1536, 1536), 1536)
        return wo_ref.at[rows, cols]

    def wop_part(i):
        return wop.at[i // 2, i % 2]

    link.send(25, w_ref.at[f], wp.at[f], here.yhi)
    link.send(26, wo_part(f), wop_part(f), here.yhi)

    def send_w(i, who, dev):
        link.send(i, wp.at[who], wp.at[who], dev)
        link.send(i + 1, wop_part(who), wop_part(who), dev)

    def wait_w(i, who, dev):
        link.wait(i, wp.at[who], dev)
        link.wait(i + 1, wop_part(who), dev)

    def half_w(i, who, half, dev, go):
        a = wp.at[who, pl.ds(96 * half, 96)]
        if go:
            link.send(i, a, a, dev)
        else:
            link.wait(i, a, dev)

    def half_wo(i, who, half, dev, go):
        b = wop.at[who // 2, who % 2, :, pl.ds(768 * half, 768)]
        if go:
            link.send(i, b, b, dev)
        else:
            link.wait(i, b, dev)

    def spread(base, dy):
        who = here.frame_at(dy, 0, 0)
        send_w(base, who, here.xp)
        send_w(base + 2, who, here.xm)
        send_w(base + 4, who, here.sib)

    def relay(base, dy):
        left, right = here.frame_at(dy, 3, 0), here.frame_at(dy, 1, 0)
        wait_w(base, left, here.xm)
        half_w(base + 6, left, 0, here.xp, True)
        half_wo(base + 7, left, 0, here.xp, True)
        send_w(base + 10, left, here.sib)
        wait_w(base + 2, right, here.xp)
        half_w(base + 8, right, 1, here.xm, True)
        half_wo(base + 9, right, 1, here.xm, True)
        send_w(base + 12, right, here.sib)

    def finish(base, dy):
        far = here.frame_at(dy, 2, 0)
        half_w(base + 6, far, 0, here.xm, False)
        half_wo(base + 7, far, 0, here.xm, False)
        half_w(base + 8, far, 1, here.xp, False)
        half_wo(base + 9, far, 1, here.xp, False)
        send_w(base + 14, far, here.sib)

    def sib_all(base, dy):
        wait_w(base + 4, here.frame_at(dy, 0, 1), here.sib)
        wait_w(base + 10, here.frame_at(dy, 3, 1), here.sib)
        wait_w(base + 12, here.frame_at(dy, 1, 1), here.sib)
        wait_w(base + 14, here.frame_at(dy, 2, 1), here.sib)

    W0, W1 = 30, 46
    wait_w(25, f, here.yhi)
    send_w(27, f, here.ylo)
    spread(W0, 0)

    for d in range(1, 16):
        peer = lax.rem(s + 16 - d, 16)
        link.wait(9 + d, modbuf.at[peer], (f, peer))
    for i in range(16):
        modrows[pl.ds(i * 9, 9), :] = modbuf[i, 0:9, :]
    even = modrows[pl.ds(0, 72, stride=2), :]
    odd = modrows[pl.ds(1, 72, stride=2), :]
    modt[...] = jnp.concatenate([even, odd], axis=1)
    gate_out[...] = modt[48:72, :]

    first = lax.broadcasted_iota(jnp.int32, (80, GROUP), 1) < HEAD
    q_scale = math.log2(math.e) / math.sqrt(HEAD)

    def normalise(raw):
        def tile(h, c):
            return raw[h, :, c * 128 : (c + 1) * 128].astype(F32)

        spots = [(h, c) for h in range(2) for c in range(6)]
        total = jnp.zeros((80, 128), F32)
        for h, c in spots:
            total = total + tile(h, c)
        mean = jnp.sum(total[:40] + total[40:], axis=-1, keepdims=True) * (1.0 / D)
        mean = jnp.concatenate([mean, mean], axis=0)
        total = jnp.zeros((80, 128), F32)
        for h, c in spots:
            diff = tile(h, c) - mean
            total = total + diff * diff
        var = jnp.sum(total[:40] + total[40:], axis=-1, keepdims=True) * (1.0 / D)
        inv = lax.rsqrt(var + 1e-05)
        inv = jnp.concatenate([inv, inv], axis=0)
        return lambda h, c: (tile(h, c) - mean) * inv

    def modulate(p, a, b):
        na, nb = normalise(blocks.at[a]), normalise(blocks.at[b])
        for h in range(2):
            for c in range(6):
                va, vb = na(h, c), nb(h, c)
                for half in range(2):
                    t = h * 12 + half * 6 + c
                    rows = slice(half * 40, half * 40 + 40)
                    both = jnp.concatenate([va[rows], vb[rows]], axis=0)
                    scale = 1.0 + modt[24 + t : 25 + t, :]
                    out = both * scale + modt[t : t + 1, :]
                    x_scr[p, t // 6, :, (t % 6) * 128 : (t % 6 + 1) * 128] = out.astype(BF)

    def project(p, weights):
        def step(k, acc):
            part = weights[pl.ds(k * 4, 4)].reshape(768, 3 * GROUP)
            return acc + jnp.dot(x_scr[p, k], part, preferred_element_type=F32)

        joined = lax.fori_loop(0, 4, step, jnp.zeros((80, 3 * GROUP), F32))
        q = head_norm_pair(joined[:, :GROUP], qg_ref[...], first) * q_scale
        k = head_norm_pair(joined[:, GROUP : 2 * GROUP], kg_ref[...], first)
        return q.astype(BF), k.astype(BF), joined[:, 2 * GROUP :].astype(BF)

    def project_own(p):
        rows = slice(p * 80, p * 80 + 80)
        q, k, v = project(p, w_ref)
        q_out[rows, :] = q
        kv_out[0, rows, :] = k
        kv_out[1, rows, :] = v

    def project_swap(p):
        q, k, v = project(p, wp)
        rows = slice(p * 80, p * 80 + 80)
        swap_out[0, rows, :] = q
        swap_out[1, rows, :] = k
        swap_out[2, rows, :] = v
        part = pl.ds(p * 80, 80)
        link.send(64 + p, swap_out.at[:, part], swap_in.at[:, part], here.yhi)

    link.wait(0, blocks.at[1], here.zm)
    link.send(2, blocks.at[1], blocks.at[3], here.zp)
    link.wait(1, blocks.at[2], here.zp)
    link.send(3, blocks.at[2], blocks.at[4], here.zm)
    wait_w(27, here.frame_at(1, 0, 0), here.ylo)
    spread(W1, 1)
    modulate(1, 1, 2)
    relay(W0, 0)
    project_own(1)

    link.wait(2, blocks.at[3], here.zm)
    link.send(4, blocks.at[3], blocks.at[5], here.zp)
    link.wait(3, blocks.at[4], here.zp)
    link.send(5, blocks.at[4], blocks.at[6], here.zm)
    relay(W1, 1)
    modulate(2, 3, 4)
    project_own(2)
    finish(W0, 0)

    link.wait(4, blocks.at[5], here.zm)
    link.send(6, blocks.at[5, 0], blocks.at[7, 0], here.zp)
    link.wait(5, blocks.at[6], here.zp)
    link.send(7, blocks.at[6, 1], blocks.at[7, 1], here.zm)
    finish(W1, 1)
    modulate(3, 5, 6)
    project_own(3)
    sib_all(W0, 0)
    sib_all(W1, 1)
    for p in (1, 2, 3):
        project_swap(p)
    link.wait(6, blocks.at[7, 0], here.zm)
    link.wait(7, blocks.at[7, 1], here.zp)
    modulate(0, 0, 7)
    project_swap(0)
    project_own(0)
    wop_out[...] = wop[...]
    for p in (1, 2, 3, 0):
        part = pl.ds(p * 80, 80)
        link.wait(64 + p, swap_in.at[:, part], here.yhi)
    q_out[320:640, :] = swap_in[0]
    kv_out[0, 320:640, :] = swap_in[1]
    kv_out[1, 320:640, :] = swap_in[2]
    link.drain()


def qkv_call(tok, mod, w, wo, qg, kg):
    vm = pl.BlockSpec(memory_space=pltpu.VMEM)
    return pl.pallas_call(
        qkv_kernel,
        out_shape=(
            jax.ShapeDtypeStruct((640, GROUP), BF),
            jax.ShapeDtypeStruct((2, 640, GROUP), BF),
            jax.ShapeDtypeStruct((8, 2, 16, 1536), BF),
            jax.ShapeDtypeStruct((24, 128), F32),
        ),
        in_specs=[vm] * 6,
        out_specs=(vm,) * 4,
        scratch_shapes=[
            pltpu.VMEM((8, 2, 80, 768), BF),
            pltpu.VMEM((16, 16, 64), F32),
            pltpu.VMEM((144, 64), F32),
            pltpu.VMEM((72, 128), F32),
            pltpu.VMEM((16, 192, 3 * GROUP), BF),
            pltpu.VMEM((8, 2, 16, 1536), BF),
            pltpu.VMEM((4, 4, 80, 768), BF),
            pltpu.VMEM((3, 320, GROUP), BF),
            pltpu.VMEM((3, 320, GROUP), BF),
            pltpu.SemaphoreType.DMA((68,)),
            pltpu.SemaphoreType.DMA((68,)),
        ],
        compiler_params=pltpu.CompilerParams(
            collective_id=0, has_side_effects=True, vmem_limit_bytes=VMEM_LIMIT
        ),
        name="qkv",
    )(tok, mod, w, wo, qg, kg)


def attend_kernel(q_ref, kv_ref, mixed_out, kv, qm, v2, acc, top, send_sem, recv_sem):
    here = Place()
    ready = meet([here.sib, here.ylo, here.xp, here.xm])
    link = Link(send_sem, recv_sem)
    kv[0] = kv_ref[...]
    lanes = lax.broadcasted_iota(jnp.int32, (640, GROUP), 1) < HEAD
    zero = jnp.zeros((640, GROUP), BF)
    qm[0] = jnp.where(lanes, q_ref[...], zero)
    qm[1] = jnp.where(lanes, zero, q_ref[...])
    acc[...] = jnp.zeros(acc.shape, F32)
    top[...] = jnp.full(top.shape, -1e30, F32)
    ready()

    R = 320

    def attend(slot):
        values = kv[slot, 1]
        one = jnp.ones((640, GROUP), BF)
        v2[0] = jnp.where(lanes, values, one)
        v2[1] = jnp.where(lanes, one, values)

        def step(i, carry):
            h, rows = i // (640 // R), pl.ds(pl.multiple_of((i % (640 // R)) * R, R), R)
            scores = lax.dot_general(
                qm[h, rows, :], kv[slot, 0], (((1,), (1,)), ((), ())),
                preferred_element_type=F32,
            )
            old = top[h, rows, :]
            new = jnp.maximum(old, jnp.max(scores, axis=1, keepdims=True))
            probs = jnp.exp2(scores - jnp.concatenate([new] * 5, axis=1)).astype(BF)
            part = jnp.dot(probs, v2[h], preferred_element_type=F32)
            acc[h, rows, :] = acc[h, rows, :] * jnp.exp2(old - new) + part
            top[h, rows, :] = new
            return carry

        lax.fori_loop(0, 2 * (640 // R), step, 0)

    def spread(base, slot):
        link.send(base, kv.at[slot], kv.at[slot + 1], here.xp)
        link.send(base + 1, kv.at[slot], kv.at[slot + 2], here.xm)
        link.send(base + 2, kv.at[slot], kv.at[slot + 8], here.sib)

    def relay(base, slot):
        link.wait(base, kv.at[slot + 1], here.xm)
        link.send(base + 3, kv.at[slot + 1, 0], kv.at[slot + 3, 0], here.xp)
        link.send(base + 5, kv.at[slot + 1], kv.at[slot + 9], here.sib)
        link.wait(base + 1, kv.at[slot + 2], here.xp)
        link.send(base + 4, kv.at[slot + 2, 1], kv.at[slot + 3, 1], here.xm)
        link.send(base + 6, kv.at[slot + 2], kv.at[slot + 10], here.sib)

    def finish(base, slot):
        link.wait(base + 3, kv.at[slot + 3, 0], here.xm)
        link.wait(base + 4, kv.at[slot + 3, 1], here.xp)
        link.send(base + 7, kv.at[slot + 3], kv.at[slot + 11], here.sib)

    def from_sib(i, slot):
        link.wait(i, kv.at[slot], here.sib)
        attend(slot)

    link.send(16, kv.at[0], kv.at[4], here.ylo)
    spread(0, 0)
    attend(0)
    from_sib(2, 8)
    link.wait(16, kv.at[4], here.ylo)
    spread(8, 4)
    attend(4)
    relay(0, 0)
    attend(1)
    attend(2)
    from_sib(10, 12)
    relay(8, 4)
    from_sib(5, 9)
    finish(0, 0)
    from_sib(6, 10)
    attend(3)
    attend(5)
    finish(8, 4)
    attend(6)
    from_sib(13, 13)
    from_sib(14, 14)
    from_sib(7, 11)
    attend(7)
    from_sib(15, 15)

    top_half = acc[0] / pltpu.roll(acc[0], HEAD, 1)
    low_half = acc[1] / pltpu.roll(acc[1], HEAD, 1)
    mixed_out[...] = jnp.where(lanes, top_half, low_half).astype(BF)
    link.drain()


def attend_call(q, kv):
    vm = pl.BlockSpec(memory_space=pltpu.VMEM)
    return pl.pallas_call(
        attend_kernel,
        out_shape=jax.ShapeDtypeStruct((640, GROUP), BF),
        in_specs=[vm] * 2,
        out_specs=vm,
        scratch_shapes=[
            pltpu.VMEM((16, 2, 640, GROUP), BF),
            pltpu.VMEM((2, 640, GROUP), BF),
            pltpu.VMEM((2, 640, GROUP), BF),
            pltpu.VMEM((2, 640, GROUP), F32),
            pltpu.VMEM((2, 640, GROUP), F32),
            pltpu.SemaphoreType.DMA((17,)),
            pltpu.SemaphoreType.DMA((17,)),
        ],
        compiler_params=pltpu.CompilerParams(
            collective_id=1, has_side_effects=True, vmem_limit_bytes=VMEM_LIMIT
        ),
        name="attend",
    )(q, kv)


def out_kernel(
    mixed_ref, wo_ref, wop_ref, tok_ref, gate_ref, fresh_ref,
    out_ref,
    w2, lhs, other, part, up, down, up_in, down_in, moved, arrived,
    send_sem, recv_sem,
):
    here = Place()
    ready = meet([here.yhi, here.zp, here.zm, here.prev, here.next])
    link = Link(send_sem, recv_sem)
    lhs[:, :GROUP] = mixed_ref[0:320, :]
    ready()
    link.send(0, mixed_ref.at[pl.ds(320, 320)], other, here.yhi)
    w2[0:128, :] = wo_ref[...]
    for h in range(2):
        w2[128:256, h * 1536 : (h + 1) * 1536] = wop_ref[:, h].reshape(128, 1536)
    link.wait(0, other, here.yhi)
    lhs[:, GROUP:] = other[...]

    def multiply(p):
        for h in range(2):
            sums = []
            for k in range(2):
                c = h * 1536 + k * 768
                sums.append(
                    jnp.dot(
                        lhs[p * 80 : p * 80 + 80, :], w2[:, c : c + 768],
                        preferred_element_type=F32,
                    )
                )
            part[0, h] = jnp.concatenate([sums[0][:40], sums[1][:40]], axis=0)
            part[1, h] = jnp.concatenate([sums[0][40:], sums[1][40:]], axis=0)

    multiply(0)
    down[0, 0] = part[1, 0].astype(BF)
    link.send(1, down.at[0, 0], down_in.at[0, 0], here.zm)
    up[0, 1] = part[1, 1].astype(BF)
    link.send(2, up.at[0, 1], up_in.at[0, 1], here.zp)
    own = [part[0, h] for h in range(2)]
    for h in range(2):
        moved[h] = own[h]

    for step, p in ((1, 3), (2, 2), (3, 1)):
        multiply(p)
        for h in ((0, 1) if step > 1 else (1, 0)):
            i = 1 + 4 * step + 2 * h
            if step == 1:
                if h == 0:
                    link.wait(1, down_in.at[0, 0], here.zp)
                else:
                    link.wait(2, up_in.at[0, 1], here.zm)
            else:
                link.wait(i - 4, down_in.at[step - 1, h], here.zp)
                link.wait(i - 3, up_in.at[step - 1, h], here.zm)
            low, high = part[0, h], part[1, h]
            if step > 1 or h == 0:
                low = low + down_in[step - 1, h].astype(F32)
            if step > 1 or h == 1:
                high = high + up_in[step - 1, h].astype(F32)
            down[step, h] = low.astype(BF)
            link.send(i, down.at[step, h], down_in.at[step, h], here.zm)
            up[step, h] = high.astype(BF)
            link.send(i + 1, up.at[step, h], up_in.at[step, h], here.zp)

    tok = to_block(tok_ref[...].astype(F32))
    for h in range(2):
        i = 13 + 2 * h
        link.wait(i, down_in.at[3, h], here.zp)
        link.wait(i + 1, up_in.at[3, h], here.zm)
        total = moved[h] + down_in[3, h].astype(F32) + up_in[3, h].astype(F32)
        pieces = []
        for c in range(6):
            cols = slice(c * 128, (c + 1) * 128)
            t = h * 12 + c
            lo = total[:40, cols] * gate_ref[t : t + 1, :]
            hi = total[40:, cols] * gate_ref[t + 6 : t + 7, :]
            pieces.append(jnp.concatenate([lo, hi], axis=0))
        arrived[0, h] = (tok[h] + jnp.concatenate(pieces, axis=1)).astype(BF)
        link.send(17 + h, arrived.at[0, h], arrived.at[1, h], here.prev)
    last = here.f == 15
    fresh = fresh_ref[...].astype(F32)
    for h in range(2):
        link.wait(17 + h, arrived.at[1, h], here.next)
        got = arrived[1, h].astype(F32)
        for k in range(2):
            cols = slice(h * 1536 + k * 768, h * 1536 + (k + 1) * 768)
            out_ref[:, cols] = jnp.where(last, fresh[:, cols], got[k * 40 : k * 40 + 40]).astype(BF)
    link.drain()


def out_call(mixed, wo, wop, tok, gate, fresh):
    vm = pl.BlockSpec(memory_space=pltpu.VMEM)
    blk = (4, 2, 80, 768)
    return pl.pallas_call(
        out_kernel,
        out_shape=jax.ShapeDtypeStruct((TOK, D), BF),
        in_specs=[vm] * 6,
        out_specs=vm,
        scratch_shapes=[
            pltpu.VMEM((256, D), BF),
            pltpu.VMEM((320, 256), BF),
            pltpu.VMEM((320, GROUP), BF),
            pltpu.VMEM((2, 2, 80, 768), F32),
            pltpu.VMEM(blk, BF),
            pltpu.VMEM(blk, BF),
            pltpu.VMEM(blk, BF),
            pltpu.VMEM(blk, BF),
            pltpu.VMEM((2, 80, 768), F32),
            pltpu.VMEM((2, 2, 80, 768), BF),
            pltpu.SemaphoreType.DMA((19,)),
            pltpu.SemaphoreType.DMA((19,)),
        ],
        compiler_params=pltpu.CompilerParams(
            collective_id=2, has_side_effects=True, vmem_limit_bytes=VMEM_LIMIT
        ),
        name="out",
    )(mixed, wo, wop, tok, gate, fresh)


def body(queue_tokens, timesteps, fresh_noise, w_mod, w_qkv, q_gain, k_gain, w_out):
    tok = queue_tokens[0]
    condition = jax.nn.silu(embed_steps(timesteps)).astype(BF)
    own = jnp.dot(condition, w_mod, preferred_element_type=F32)
    mod = jnp.pad(own.reshape(9, 64), ((0, 7), (0, 0)))
    w = w_qkv.reshape(16, 192, 3 * GROUP)
    qg = jnp.concatenate([q_gain, q_gain])[None]
    kg = jnp.concatenate([k_gain, k_gain])[None]
    q, kv, wop, gate = qkv_call(tok, mod, w, w_out, qg, kg)
    mixed = attend_call(q, kv)
    return out_call(mixed, w_out, wop, tok, gate, fresh_noise)[None]


def solution(mesh):
    return jax.shard_map(
        body,
        mesh=mesh,
        in_specs=(
            P("frame", "seq", None),
            P("frame"),
            P("seq", None),
            P(None, "seq"),
            P(None, None, "seq"),
            P(),
            P(),
            P("seq", None),
        ),
        out_specs=P("frame", "seq", None),
        check_vma=False,
    )
```

time: 523 us -> 158 us (0.30)
  waiting for transfers between devices: 355 us -> 0 us
  Pallas kernels: 0 us -> 140 us
  blocking collectives: 66.8 us -> 0 us
  matrix products: 35.3 us -> 0.32 us
  other arithmetic: 15.6 us -> 0.72 us
  between operations: 14.7 us -> 0.76 us
  local copies, waits for them, and re-layouts: 27 us -> 15.4 us
  starting transfers between devices: 7.09 us -> 0 us
    reduce_scatter x1 -> x0, waiting for transfers between devices: 208 us -> none  [body(): lax.psum_scatter(lax.optimization_barrier(term.astype(jnp.bfloat16)).asty...]
    all_gather x2 -> x0, waiting for transfers between devices: 142 us -> none  [the longest x1 101 us: body(): shard_rows = lax.all_gather(modded, 'seq', axis=0, tiled=True)]
    pallas_call x0 -> x3, Pallas kernels: none -> 140 us  [the longest x1 51.6 us: qkv_call(): pl.pallas_call(qkv_kernel, out_shape=(jax.ShapeDtypeStruct((640, GROUP),...]
    unnamed x1 -> x0, blocking collectives: 66.8 us -> none
    dot_general x13 -> x1, matrix products: 35.3 us -> 0.32 us  [body(): own = jnp.dot(condition, w_mod, preferred_element_type=F32)]
    reshape x0 -> x2, local copies, waits for them, and re-layouts: none -> 12.8 us  [body(): w = w_qkv.reshape(16, 192, 3 * GROUP)]
    reduce_sum x9 -> x0, other arithmetic: 11.7 us -> none  [the longest x5 9.28 us: one_block(): summed = jnp.sum(exponent, axis=(2, 3), keepdims=True)]
    slice x5 -> x0, local copies, waits for them, and re-layouts: 11.5 us -> none  [the longest x2 8.92 us: body(): every_frame[:, :, group_width:]]
  transfers between devices with their start and end apart: 4 -> 0, of which waited for: 4 -> 0; matrix products, arithmetic and copies ran while one was open for 1% -> 0% of each run, Pallas kernels for 0% -> 0%
where the time goes in v1:
time: 158 us; the launch traced here: 157 us
  Pallas kernels  140 us (89%)
  local copies, waits for them, and re-layouts  15.4 us (10%)
    pallas_call x1, Pallas kernels, qkv_call(): pl.pallas_call(qkv_kernel, out_shape=(jax.ShapeDtypeStruct((640, GROUP),...  51.6 us
    pallas_call x1, Pallas kernels, attend_call(): pl.pallas_call(attend_kernel, out_shape=jax.ShapeDtypeStruct((640, GROUP)...  51 us
    pallas_call x1, Pallas kernels, out_call(): pl.pallas_call(out_kernel, out_shape=jax.ShapeDtypeStruct((TOK, D), BF),...  37.6 us
    reshape x2, local copies, waits for them, and re-layouts, body(): w = w_qkv.reshape(16, 192, 3 * GROUP)  12.8 us

profile of v1, /device:TPU:1, one launch (start us, length us, event | category | flops | bytes accessed | tf_op | source)
XLA Modules:
  0.0 157.4 jit_solution(1393532787826426211)
XLA Ops:
  0.0 0.0 copy-start
  0.8 0.3 copy-done
  1.1 0.3 fusion.3
  1.4 0.6 pad.4.mod_ref
  2.0 5.7 %copy.13 = bf16[3072,3,128]{2,1,0:T(4,128)(2,1)} copy(bf16[3072,3,128]{2,0,1:T(8,128)(2,1)} %param.12) | data formatting | bytes 4718592 | tf_op jit(solution)/shard_map/reshape | solution.py:586
  7.7 0.0 copy-start.1
  7.7 0.0 copy-start.2
  7.7 7.2 %reshape.41.w_ref = bf16[16,192,384]{2,1,0:T(8,128)(2,1)} reshape(bf16[3072,3,128]{2,1,0:T(4,128)(2,1)} %copy.13) | data formatting | bytes 4718592 | tf_op jit(solution)/shard_map/reshape | solution.py:586
  14.9 0.0 copy-done.1
  14.9 0.0 copy-done.2
  14.9 0.7 maximum_bitcast_fusion
  15.5 51.6 %qkv.1 = (bf16[640,128]{1,0:T(8,128)(2,1)}, bf16[2,640,128]{2,1,0:T(8,128)(2,1)}, bf16[8,2,16,1536]{3,2,1,0:T(8,128)(2,1)}, f32[24,128]{1,0:T(8,128)}) custom-call(bf16[40,3072]{1,0:T(8,128)(2,1)} %bitcast.16, f32[16,64]{1,0:T(8,128)} %pad.4.mod_ref, bf16[16,192,384]{2,1,0:T(8,128)(2,1)} %reshape.41.w_ref, bf16[128,3072]{1,0:T(8,128)(2,1)} %wo_ref.3, ...), custom_call_target="tpu_custom_call" | custom-call | tf_op jit(solution)/shard_map/qkv/pallas_call | solution.py:320
  67.1 51.0 %attend.1.mixed_ref = bf16[640,128]{1,0:T(8,128)(2,1)} custom-call(bf16[640,128]{1,0:T(8,128)(2,1)} %get-tuple-element.9.q_ref, bf16[2,640,128]{2,1,0:T(8,128)(2,1)} %get-tuple-element.10.kv_ref), custom_call_target="tpu_custom_call" | custom-call | tf_op jit(solution)/shard_map/attend/pallas_call | solution.py:442
  118.1 37.6 %out.1 = bf16[40,3072]{1,0:T(8,128)(2,1)} custom-call(bf16[640,128]{1,0:T(8,128)(2,1)} %attend.1.mixed_ref, bf16[128,3072]{1,0:T(8,128)(2,1)} %wo_ref.3, bf16[8,2,16,1536]{3,2,1,0:T(8,128)(2,1)} %get-tuple-element.11.wop_ref, bf16[40,3072]{1,0:T(8,128)(2,1)} %bitcast.17, f32[24,128]{1,0:T(8,128)} %get-tuple-element.12.gate_ref, bf16[40,3072]{1,0:T(8,128)(2,1)} %fresh_ref.1), custom_call_target="tpu_custom_call" | custom-call | tf_op jit(solution)/shard_map/out/pallas_call | solution.py:555
  155.7 1.7 %copy.19 = bf16[1,40,3072]{2,1,0:T(8,128)(2,1)} copy(bf16[1,40,3072]{2,1,0:T(8,128)(2,1)} %bitcast.18) | data formatting | bytes 491520
  (4 shorter events, 0.1 us)
Async XLA Ops:
  0.0 1.1 copy-start
  7.7 7.2 %copy-start.1 = (f32[64]{0:T(128)S(1)}, f32[64]{0:T(128)}, u32[]{:S(2)}) copy-start(f32[64]{0:T(128)} %param.13) | copy-start | bytes 772
  7.7 7.2 %copy-start.2 = (f32[64]{0:T(128)S(1)}, f32[64]{0:T(128)}, u32[]{:S(2)}) copy-start(f32[64]{0:T(128)} %param.14) | copy-start | bytes 772

commit v2 on v1

--- a/solution.py
+++ b/solution.py
@@ -59,6 +59,7 @@
         self.sent = []
 
     def _copy(self, i, src, dst, dev):
+        src, dst = (ref() if callable(ref) else ref for ref in (src, dst))
         return pltpu.make_async_remote_copy(
             src_ref=src,
             dst_ref=dst,
@@ -69,16 +70,15 @@
         )
 
     def send(self, i, src, dst, dev):
-        copy = self._copy(i, src, dst, dev)
-        copy.start()
-        self.sent.append(copy)
+        self._copy(i, src, dst, dev).start()
+        self.sent.append((i, src, dst, dev))
 
     def wait(self, i, dst, dev):
         self._copy(i, dst, dst, dev).wait_recv()
 
     def drain(self):
-        for copy in self.sent:
-            copy.wait_send()
+        for sent in self.sent:
+            self._copy(*sent).wait_send()
 
 
 def meet(devices):
@@ -138,19 +138,19 @@
     def wop_part(i):
         return wop.at[i // 2, i % 2]
 
-    link.send(25, w_ref.at[f], wp.at[f], here.yhi)
+    link.send(25, w_ref.at[:, f], wp.at[:, f], here.yhi)
     link.send(26, wo_part(f), wop_part(f), here.yhi)
 
     def send_w(i, who, dev):
-        link.send(i, wp.at[who], wp.at[who], dev)
+        link.send(i, wp.at[:, who], wp.at[:, who], dev)
         link.send(i + 1, wop_part(who), wop_part(who), dev)
 
     def wait_w(i, who, dev):
-        link.wait(i, wp.at[who], dev)
+        link.wait(i, wp.at[:, who], dev)
         link.wait(i + 1, wop_part(who), dev)
 
     def half_w(i, who, half, dev, go):
-        a = wp.at[who, pl.ds(96 * half, 96)]
+        a = wp.at[:, who, pl.ds(96 * half, 96)]
         if go:
             link.send(i, a, a, dev)
         else:
@@ -246,7 +246,9 @@
 
     def project(p, weights):
         def step(k, acc):
-            part = weights[pl.ds(k * 4, 4)].reshape(768, 3 * GROUP)
+            part = jnp.concatenate(
+                [weights[j, pl.ds(k * 4, 4)].reshape(768, GROUP) for j in range(3)], axis=1
+            )
             return acc + jnp.dot(x_scr[p, k], part, preferred_element_type=F32)
 
         joined = lax.fori_loop(0, 4, step, jnp.zeros((80, 3 * GROUP), F32))
@@ -332,7 +334,7 @@
             pltpu.VMEM((16, 16, 64), F32),
             pltpu.VMEM((144, 64), F32),
             pltpu.VMEM((72, 128), F32),
-            pltpu.VMEM((16, 192, 3 * GROUP), BF),
+            pltpu.VMEM((3, 16, 192, GROUP), BF),
             pltpu.VMEM((8, 2, 16, 1536), BF),
             pltpu.VMEM((4, 4, 80, 768), BF),
             pltpu.VMEM((3, 320, GROUP), BF),
@@ -347,93 +349,113 @@
     )(tok, mod, w, wo, qg, kg)
 
 
-def attend_kernel(q_ref, kv_ref, mixed_out, kv, qm, v2, acc, top, send_sem, recv_sem):
+ORDER = [
+    (0, 0, 0), (1, 0, 0), (0, 1, 0), (0, 0, 3), (0, 0, 1), (1, 1, 0), (1, 0, 3), (1, 0, 1),
+    (0, 1, 3), (0, 1, 1), (0, 0, 2), (1, 1, 3), (1, 1, 1), (1, 0, 2), (0, 1, 2), (1, 1, 2),
+]
+SLOT = {place: i for i, place in enumerate(ORDER)}
+QCOLS = 128
+
+
+def attend_kernel(q_ref, kv_ref, mixed_out, kbuf, vbuf, qm, vt, acc, top, send_sem, recv_sem):
     here = Place()
     ready = meet([here.sib, here.ylo, here.xp, here.xm])
     link = Link(send_sem, recv_sem)
-    kv[0] = kv_ref[...]
+    kbuf[0] = kv_ref[0]
+    vbuf[0] = kv_ref[1].T
     lanes = lax.broadcasted_iota(jnp.int32, (640, GROUP), 1) < HEAD
     zero = jnp.zeros((640, GROUP), BF)
-    qm[0] = jnp.where(lanes, q_ref[...], zero)
-    qm[1] = jnp.where(lanes, zero, q_ref[...])
+    qm[0:640] = jnp.where(lanes, q_ref[...], zero)
+    qm[640:1280] = jnp.where(lanes, zero, q_ref[...])
     acc[...] = jnp.zeros(acc.shape, F32)
     top[...] = jnp.full(top.shape, -1e30, F32)
     ready()
 
-    R = 320
+    upper = lax.broadcasted_iota(jnp.int32, (GROUP, 640), 0) < HEAD
 
     def attend(slot):
-        values = kv[slot, 1]
-        one = jnp.ones((640, GROUP), BF)
-        v2[0] = jnp.where(lanes, values, one)
-        v2[1] = jnp.where(lanes, one, values)
-
-        def step(i, carry):
-            h, rows = i // (640 // R), pl.ds(pl.multiple_of((i % (640 // R)) * R, R), R)
+        one = jnp.ones((GROUP, 640), BF)
+        vt[0] = jnp.where(upper, vbuf[slot], one)
+        vt[1] = jnp.where(upper, one, vbuf[slot])
+
+        def mix(cols, head, probs, shrink):
+            part = jnp.dot(vt[head], probs, preferred_element_type=F32)
+            acc[:, cols] = acc[:, cols] * shrink + part
+
+        for n in range(1280 // QCOLS):
+            cols = slice(n * QCOLS, (n + 1) * QCOLS)
             scores = lax.dot_general(
-                qm[h, rows, :], kv[slot, 0], (((1,), (1,)), ((), ())),
-                preferred_element_type=F32,
+                kbuf[slot], qm[cols, :], (((1,), (1,)), ((), ())), preferred_element_type=F32
             )
-            old = top[h, rows, :]
-            new = jnp.maximum(old, jnp.max(scores, axis=1, keepdims=True))
-            probs = jnp.exp2(scores - jnp.concatenate([new] * 5, axis=1)).astype(BF)
-            part = jnp.dot(probs, v2[h], preferred_element_type=F32)
-            acc[h, rows, :] = acc[h, rows, :] * jnp.exp2(old - new) + part
-            top[h, rows, :] = new
-            return carry
-
-        lax.fori_loop(0, 2 * (640 // R), step, 0)
-
-    def spread(base, slot):
-        link.send(base, kv.at[slot], kv.at[slot + 1], here.xp)
-        link.send(base + 1, kv.at[slot], kv.at[slot + 2], here.xm)
-        link.send(base + 2, kv.at[slot], kv.at[slot + 8], here.sib)
-
-    def relay(base, slot):
-        link.wait(base, kv.at[slot + 1], here.xm)
-        link.send(base + 3, kv.at[slot + 1, 0], kv.at[slot + 3, 0], here.xp)
-        link.send(base + 5, kv.at[slot + 1], kv.at[slot + 9], here.sib)
-        link.wait(base + 1, kv.at[slot + 2], here.xp)
-        link.send(base + 4, kv.at[slot + 2, 1], kv.at[slot + 3, 1], here.xm)
-        link.send(base + 6, kv.at[slot + 2], kv.at[slot + 10], here.sib)
-
-    def finish(base, slot):
-        link.wait(base + 3, kv.at[slot + 3, 0], here.xm)
-        link.wait(base + 4, kv.at[slot + 3, 1], here.xp)
-        link.send(base + 7, kv.at[slot + 3], kv.at[slot + 11], here.sib)
-
-    def from_sib(i, slot):
-        link.wait(i, kv.at[slot], here.sib)
-        attend(slot)
-
-    link.send(16, kv.at[0], kv.at[4], here.ylo)
-    spread(0, 0)
-    attend(0)
-    from_sib(2, 8)
-    link.wait(16, kv.at[4], here.ylo)
-    spread(8, 4)
-    attend(4)
-    relay(0, 0)
-    attend(1)
-    attend(2)
-    from_sib(10, 12)
-    relay(8, 4)
-    from_sib(5, 9)
-    finish(0, 0)
-    from_sib(6, 10)
-    attend(3)
-    attend(5)
-    finish(8, 4)
-    attend(6)
-    from_sib(13, 13)
-    from_sib(14, 14)
-    from_sib(7, 11)
-    attend(7)
-    from_sib(15, 15)
-
-    top_half = acc[0] / pltpu.roll(acc[0], HEAD, 1)
-    low_half = acc[1] / pltpu.roll(acc[1], HEAD, 1)
-    mixed_out[...] = jnp.where(lanes, top_half, low_half).astype(BF)
+            old = top[0:1, cols]
+            new = jnp.maximum(old, jnp.max(scores, axis=0, keepdims=True))
+            probs = jnp.exp2(scores - new).astype(BF)
+            top[0:1, cols] = new
+            mix(cols, n * QCOLS // 640, probs, jnp.exp2(old - new))
+
+    def block(kind, place):
+        return lambda: (kbuf, vbuf)[kind].at[SLOT[place]]
+
+    def send(src, dst, dev, kinds=(0, 1)):
+        for kind in kinds:
+            link.send(2 * SLOT[dst] + kind, block(kind, src), block(kind, dst), dev)
+
+    def wait(dst, kinds=(0, 1)):
+        for kind in kinds:
+            link.wait(2 * SLOT[dst] + kind, block(kind, dst), here.sib)
+
+    def spread(y):
+        send((0, y, 0), (0, y, 3), here.xp)
+        send((0, y, 0), (0, y, 1), here.xm)
+        send((0, y, 0), (1, y, 0), here.sib)
+
+    def relay(y):
+        wait((0, y, 3))
+        send((0, y, 3), (0, y, 2), here.xp, (0,))
+        send((0, y, 3), (1, y, 3), here.sib)
+        wait((0, y, 1))
+        send((0, y, 1), (0, y, 2), here.xm, (1,))
+        send((0, y, 1), (1, y, 1), here.sib)
+
+    def finish(y):
+        wait((0, y, 2))
+        send((0, y, 2), (1, y, 2), here.sib)
+
+    def arrive_y():
+        wait((0, 1, 0))
+        spread(1)
+
+    events = {
+        0: [lambda: send((0, 0, 0), (0, 1, 0), here.ylo), lambda: spread(0)],
+        1: [lambda: wait(ORDER[1])],
+        2: [arrive_y, lambda: relay(0)],
+        5: [lambda: wait(ORDER[5])],
+        6: [lambda: wait(ORDER[6])],
+        7: [lambda: wait(ORDER[7])],
+        8: [lambda: relay(1)],
+        10: [lambda: finish(0)],
+        11: [lambda: wait(ORDER[11])],
+        12: [lambda: wait(ORDER[12])],
+        13: [lambda: wait(ORDER[13])],
+        14: [lambda: finish(1)],
+        15: [lambda: wait(ORDER[15])],
+    }
+
+    def step(t, carry):
+        for when, acts in events.items():
+
+            @pl.when(t == when)
+            def _():
+                for act in acts:
+                    act()
+
+        attend(t)
+        return carry
+
+    lax.fori_loop(0, 16, step, 0)
+    first = acc[0:64, 0:640] / acc[64:65, 0:640]
+    second = acc[64:128, 640:1280] / acc[0:1, 640:1280]
+    mixed_out[...] = jnp.concatenate([first, second], axis=0).T.astype(BF)
     link.drain()
 
 
@@ -445,13 +467,14 @@
         in_specs=[vm] * 2,
         out_specs=vm,
         scratch_shapes=[
-            pltpu.VMEM((16, 2, 640, GROUP), BF),
-            pltpu.VMEM((2, 640, GROUP), BF),
-            pltpu.VMEM((2, 640, GROUP), BF),
-            pltpu.VMEM((2, 640, GROUP), F32),
-            pltpu.VMEM((2, 640, GROUP), F32),
-            pltpu.SemaphoreType.DMA((17,)),
-            pltpu.SemaphoreType.DMA((17,)),
+            pltpu.VMEM((16, 640, GROUP), BF),
+            pltpu.VMEM((16, GROUP, 640), BF),
+            pltpu.VMEM((1280, GROUP), BF),
+            pltpu.VMEM((2, GROUP, 640), BF),
+            pltpu.VMEM((GROUP, 1280), F32),
+            pltpu.VMEM((8, 1280), F32),
+            pltpu.SemaphoreType.DMA((32,)),
+            pltpu.SemaphoreType.DMA((32,)),
         ],
         compiler_params=pltpu.CompilerParams(
             collective_id=1, has_side_effects=True, vmem_limit_bytes=VMEM_LIMIT
@@ -583,7 +606,7 @@
     condition = jax.nn.silu(embed_steps(timesteps)).astype(BF)
     own = jnp.dot(condition, w_mod, preferred_element_type=F32)
     mod = jnp.pad(own.reshape(9, 64), ((0, 7), (0, 0)))
-    w = w_qkv.reshape(16, 192, 3 * GROUP)
+    w = jnp.transpose(w_qkv, (1, 0, 2)).reshape(3, 16, 192, GROUP)
     qg = jnp.concatenate([q_gain, q_gain])[None]
     kg = jnp.concatenate([k_gain, k_gain])[None]
     q, kv, wop, gate = qkv_call(tok, mod, w, w_out, qg, kg)

time: 158 us -> 129 us (0.82)
  Pallas kernels: 140 us -> 122 us
  local copies, waits for them, and re-layouts: 15.4 us -> 2.65 us
    pallas_call x1, Pallas kernels: 51 us -> 35.6 us  [attend_call(): pl.pallas_call(attend_kernel, out_shape=jax.ShapeDtypeStruct((640, GROUP)...]
    reshape x2 -> x0, local copies, waits for them, and re-layouts: 12.8 us -> none  [body(): w = w_qkv.reshape(16, 192, 3 * GROUP)]
    pallas_call x1, Pallas kernels: 37.6 us -> 34.9 us  [out_call(): pl.pallas_call(out_kernel, out_shape=jax.ShapeDtypeStruct((TOK, D), BF),...]
where the time goes in v2:
time: 129 us; the launch traced here: 127 us
  Pallas kernels  122 us (95%)
  local copies, waits for them, and re-layouts  2.65 us (2%)
  other arithmetic  1.45 us (1%)
    pallas_call x1, Pallas kernels, qkv_call(): pl.pallas_call(qkv_kernel, out_shape=(jax.ShapeDtypeStruct((640, GROUP),...  51.6 us
    pallas_call x1, Pallas kernels, attend_call(): pl.pallas_call(attend_kernel, out_shape=jax.ShapeDtypeStruct((640, GROUP)...  35.6 us
    pallas_call x1, Pallas kernels, out_call(): pl.pallas_call(out_kernel, out_shape=jax.ShapeDtypeStruct((TOK, D), BF),...  34.9 us

profile of v2, /device:TPU:1, one launch (start us, length us, event | category | flops | bytes accessed | tf_op | source)
XLA Modules:
  0.0 127.3 jit_solution(4218482671559542654)
XLA Ops:
  0.0 0.0 copy-start
  0.7 0.4 copy-done
  1.1 1.4 %maximum_bitcast_fusion = (f32[1,128]{1,0:T(1,128)}, f32[1,128]{1,0:T(1,128)}) fusion(f32[64]{0:T(128)} %param.13, f32[64]{0:T(128)} %param.14), kind=kLoop, calls=%fused_computation.7 | loop fusion | flops 256 | bytes 1536 | tf_op jit(solution)/shard_map/broadcast_in_dim | solution.py:610
  2.6 0.3 fusion.3
  2.9 0.6 pad.4.mod_ref
  3.5 51.6 %qkv.1 = (bf16[640,128]{1,0:T(8,128)(2,1)}, bf16[2,640,128]{2,1,0:T(8,128)(2,1)}, bf16[8,2,16,1536]{3,2,1,0:T(8,128)(2,1)}, f32[24,128]{1,0:T(8,128)}) custom-call(bf16[40,3072]{1,0:T(8,128)(2,1)} %bitcast.20, f32[16,64]{1,0:T(8,128)} %pad.4.mod_ref, bf16[3,16,192,128]{3,2,1,0:T(8,128)(2,1)} %bitcast.19, bf16[128,3072]{1,0:T(8,128)(2,1)} %wo_ref.3, ...), custom_call_target="tpu_custom_call" | custom-call | tf_op jit(solution)/shard_map/qkv/pallas_call | solution.py:322
  55.1 35.6 %attend.1.mixed_ref = bf16[640,128]{1,0:T(8,128)(2,1)} custom-call(bf16[640,128]{1,0:T(8,128)(2,1)} %get-tuple-element.9.q_ref, bf16[2,640,128]{2,1,0:T(8,128)(2,1)} %get-tuple-element.10.kv_ref), custom_call_target="tpu_custom_call" | custom-call | tf_op jit(solution)/shard_map/attend/pallas_call | solution.py:464
  90.7 34.9 %out.1 = bf16[40,3072]{1,0:T(8,128)(2,1)} custom-call(bf16[640,128]{1,0:T(8,128)(2,1)} %attend.1.mixed_ref, bf16[128,3072]{1,0:T(8,128)(2,1)} %wo_ref.3, bf16[8,2,16,1536]{3,2,1,0:T(8,128)(2,1)} %get-tuple-element.11.wop_ref, bf16[40,3072]{1,0:T(8,128)(2,1)} %bitcast.21, f32[24,128]{1,0:T(8,128)} %get-tuple-element.12.gate_ref, bf16[40,3072]{1,0:T(8,128)(2,1)} %fresh_ref.1), custom_call_target="tpu_custom_call" | custom-call | tf_op jit(solution)/shard_map/out/pallas_call | solution.py:578
  125.6 1.7 %copy.14 = bf16[1,40,3072]{2,1,0:T(8,128)(2,1)} copy(bf16[1,40,3072]{2,1,0:T(8,128)(2,1)} %bitcast.22) | data formatting | bytes 491520
  (4 shorter events, 0.1 us)
Async XLA Ops:
  0.0 1.1 copy-start

commit v3 on v0

v3 whole, which is shorter than its diff:
```python
import math

import jax
import jax.numpy as jnp
from jax import lax
from jax.experimental import pallas as pl
from jax.experimental.pallas import tpu as pltpu
from jax.sharding import PartitionSpec as P

TEMB = 512
TOK = 40
D = 3072
GROUP = 128
HEAD = 64
BF = jnp.bfloat16
F32 = jnp.float32
MESH = pl.DeviceIdType.MESH
VMEM_LIMIT = 56 * 1024 * 1024


def embed_steps(levels):
    halfway = TEMB // 2
    frequency = jnp.exp(-math.log(10000.0) * jnp.arange(halfway, dtype=F32) / halfway)
    angles = levels.astype(F32)[:, None] * frequency[None, :]
    return jnp.concatenate([jnp.cos(angles), jnp.sin(angles)], axis=-1)


class Place:
    def __init__(self):
        f = lax.axis_index("frame")
        s = lax.axis_index("seq")
        self.f, self.s = f, s
        ylo, x, core = f // 8, (f // 2) % 4, f % 2
        yhi, z = s // 8, s % 8
        self.core, self.z, self.yhi_at = core, z, yhi
        self.zs = {d: (z + d + 8) % 8 for d in range(-4, 5)}
        self.coords = (ylo, x, core)
        self.sib = (self.frame_at(0, 0, 1), s)
        self.ylo = (self.frame_at(1, 0, 0), s)
        self.xp = (self.frame_at(0, 1, 0), s)
        self.xm = (self.frame_at(0, 3, 0), s)
        self.zp = self.along_z(1)
        self.zm = self.along_z(-1)
        self.yhi = (f, (1 - yhi) * 8 + z)
        self.prev = ((f + 15) % 16, s)
        self.next = ((f + 1) % 16, s)
        self.far = ((f + 15 + 2 * core) % 16, s)

    def frame_at(self, dy, dx, dc):
        ylo, x, core = self.coords
        return (ylo + dy) % 2 * 8 + (x + dx) % 4 * 2 + (core + dc) % 2

    def z_at(self, d):
        return self.zs[d]

    def along_z(self, d):
        return (self.f, self.yhi_at * 8 + self.z_at(d))


class Link:
    def __init__(self, send_sem, recv_sem):
        self.send_sem, self.recv_sem = send_sem, recv_sem
        self.ids = {}
        self.sent = []

    def _copy(self, name, src, dst, dev):
        i = self.ids.setdefault(name, len(self.ids))
        return pltpu.make_async_remote_copy(
            src_ref=src(),
            dst_ref=dst(),
            send_sem=self.send_sem.at[i],
            recv_sem=self.recv_sem.at[i],
            device_id=dev,
            device_id_type=MESH,
        )

    def send(self, name, src, dst, dev):
        self._copy(name, src, dst, dev).start()
        self.sent.append((name, src, dst, dev))

    def wait(self, name, dst, dev):
        self._copy(name, dst, dst, dev).wait_recv()

    def drain(self):
        for sent in self.sent:
            self._copy(*sent).wait_send()


def meet(devices):
    barrier = pltpu.get_barrier_semaphore()
    for dev in devices:
        pl.semaphore_signal(barrier, inc=1, device_id=dev, device_id_type=MESH)
    return lambda: pl.semaphore_wait(barrier, len(devices))


def to_block(rows):
    pieces = []
    for h in range(2):
        lo = rows[:, h * 1536 : h * 1536 + 768]
        hi = rows[:, h * 1536 + 768 : (h + 1) * 1536]
        pieces.append(jnp.concatenate([lo, hi], axis=0))
    return pieces


def head_norm_pair(x, gain, first):
    a = jnp.sum(jnp.where(first, x, 0.0), axis=-1, keepdims=True) * (1.0 / HEAD)
    b = jnp.sum(jnp.where(first, 0.0, x), axis=-1, keepdims=True) * (1.0 / HEAD)
    c = x - jnp.where(first, a, b)
    sq = c * c
    va = jnp.sum(jnp.where(first, sq, 0.0), axis=-1, keepdims=True) * (1.0 / HEAD)
    vb = jnp.sum(jnp.where(first, 0.0, sq), axis=-1, keepdims=True) * (1.0 / HEAD)
    return c * lax.rsqrt(jnp.where(first, va, vb) + 1e-06) * gain


N_COPIES = 176


def layer_kernel(
    tok_ref, mod_ref, w_ref, wo_ref, qg_ref, kg_ref, fresh_ref,
    out_ref,
    blocks, modbuf, modt, wp, x_scr, swap, qin, kv, qm, vt, acc, top,
    wz, mixed, outbox, lhs, own_part, give, take_in, moved, arrived,
    send_sem, recv_sem,
):
    here = Place()
    f, s, z, core = here.f, here.s, here.z, here.core
    seq_peers = [(f, lax.rem(s + d, 16)) for d in range(1, 16)]
    ready = meet(seq_peers + [here.sib, here.ylo, here.xp, here.xm, here.far])
    link = Link(send_sem, recv_sem)

    tok = tok_ref[...].astype(F32)
    for h, piece in enumerate(to_block(tok)):
        blocks[0, h] = piece.astype(BF)
    modbuf[s] = mod_ref[...]
    for c in range(2):
        for h in range(2):
            wz[z, c, h] = wo_ref[c * 64 : (c + 1) * 64, h * 1536 : (h + 1) * 1536]
    acc[...] = jnp.zeros(acc.shape, F32)
    top[...] = jnp.full(top.shape, -1e30, F32)
    ready()

    for d, dev in enumerate(seq_peers):
        link.send(("mod", d + 1), lambda: modbuf.at[s], lambda: modbuf.at[s], dev)

    def send_tok(j):
        src = (0, 1, 3)[j], (0, 2, 4)[j]
        dst = (1, 3, 5)[j], (2, 4, 6)[j]
        link.send(("up", j), lambda: blocks.at[src[0]], lambda: blocks.at[dst[0]], here.zp)
        link.send(("down", j), lambda: blocks.at[src[1]], lambda: blocks.at[dst[1]], here.zm)

    def wait_tok(j):
        dst = (1, 3, 5)[j], (2, 4, 6)[j]
        link.wait(("up", j), lambda: blocks.at[dst[0]], here.zm)
        link.wait(("down", j), lambda: blocks.at[dst[1]], here.zp)

    send_tok(0)
    link.send("w", lambda: w_ref.at[:, f], lambda: wp.at[:, f], here.yhi)

    def slice_of(who, half=None):
        if half is None:
            return lambda: wp.at[:, who]
        return lambda: wp.at[:, who, pl.ds(96 * half, 96)]

    def w_send(name, who, dev, half=None):
        link.send(("w", name), slice_of(who, half), slice_of(who, half), dev)

    def w_wait(name, who, half=None):
        link.wait(("w", name), slice_of(who, half), here.sib)

    def w_spread(y):
        who = here.frame_at(y, 0, 0)
        w_send((y, "xp"), who, here.xp)
        w_send((y, "xm"), who, here.xm)
        w_send((y, "s0"), who, here.sib)

    def w_relay(y):
        left, right = here.frame_at(y, 3, 0), here.frame_at(y, 1, 0)
        w_wait((y, "xp"), left)
        w_send((y, "xp2"), left, here.xp, 0)
        w_send((y, "s3"), left, here.sib)
        w_wait((y, "xm"), right)
        w_send((y, "xm2"), right, here.xm, 1)
        w_send((y, "s1"), right, here.sib)

    def w_finish(y):
        far = here.frame_at(y, 2, 0)
        w_wait((y, "xp2"), far, 0)
        w_wait((y, "xm2"), far, 1)
        w_send((y, "s2"), far, here.sib)

    def w_from_sib(y):
        for dx in range(4):
            w_wait((y, f"s{dx}"), here.frame_at(y, dx, 1))

    def wo_at(zz, c, h):
        return lambda: wz.at[zz, c, h]

    def wo_start():
        rows = pl.ds(pl.multiple_of(core * 64, 64), 64)
        for h in range(2):
            src = lambda h=h: wo_ref.at[rows, pl.ds(h * 1536, 1536)]
            link.send(("wo", "up", 1, h), src, wo_at(z, core, h), here.zp)
            link.send(("wo", "down", 1, h), src, wo_at(z, core, h), here.zm)

    def wo_relay(d, h):
        for way, zz, dev, last in (("up", here.z_at(-d), here.zp, 0), ("down", here.z_at(d), here.zm, 1)):
            if d == 4 and h != last:
                continue
            at = wo_at(zz, core, h)
            link.wait(("wo", way, d, h), at, dev)
            if d < 3 or (d == 3 and h == last):
                link.send(("wo", way, d + 1, h), at, at, dev)
            link.send(("wo", "sib", way, d, h), at, at, here.sib)

    def wo_from_sib(d, h):
        for way, zz, last in (("up", here.z_at(-d), 0), ("down", here.z_at(d), 1)):
            if d == 4 and h != last:
                continue
            link.wait(("wo", "sib", way, d, h), wo_at(zz, 1 - core, h), here.sib)

    first = lax.broadcasted_iota(jnp.int32, (1, GROUP), 1) < HEAD
    q_scale = math.log2(math.e) / math.sqrt(HEAD)

    def normalise(raw):
        def tile(h, c):
            return raw[h, :, c * 128 : (c + 1) * 128].astype(F32)

        spots = [(h, c) for h in range(2) for c in range(6)]
        total = jnp.zeros((80, 128), F32)
        for h, c in spots:
            total = total + tile(h, c)
        mean = jnp.sum(total[:40] + total[40:], axis=-1, keepdims=True) * (1.0 / D)
        mean = jnp.concatenate([mean, mean], axis=0)
        total = jnp.zeros((80, 128), F32)
        for h, c in spots:
            diff = tile(h, c) - mean
            total = total + diff * diff
        var = jnp.sum(total[:40] + total[40:], axis=-1, keepdims=True) * (1.0 / D)
        inv = lax.rsqrt(var + 1e-05)
        inv = jnp.concatenate([inv, inv], axis=0)
        return lambda h, c: (tile(h, c) - mean) * inv

    def modulate(p, a, b):
        na, nb = normalise(blocks.at[a]), normalise(blocks.at[b])
        for h in range(2):
            for c in range(6):
                va, vb = na(h, c), nb(h, c)
                for half in range(2):
                    t = h * 12 + half * 6 + c
                    rows = slice(half * 40, half * 40 + 40)
                    both = jnp.concatenate([va[rows], vb[rows]], axis=0)
                    scale = 1.0 + modt[24 + t : 25 + t, :]
                    out = both * scale + modt[t : t + 1, :]
                    x_scr[p, t // 6, :, (t % 6) * 128 : (t % 6 + 1) * 128] = out.astype(BF)

    def project(p, n, weights):
        def step(k, total):
            part = jnp.concatenate(
                [weights[j, pl.ds(k * 4, 4)].reshape(768, GROUP) for j in range(3)], axis=1
            )
            rows = x_scr[p : p + n, k].reshape(n * 80, 768)
            return total + jnp.dot(rows, part, preferred_element_type=F32)

        joined = lax.fori_loop(0, 4, step, jnp.zeros((n * 80, 3 * GROUP), F32))
        q = head_norm_pair(joined[:, :GROUP], qg_ref[...], first) * q_scale
        k = head_norm_pair(joined[:, GROUP : 2 * GROUP], kg_ref[...], first)
        return q.astype(BF), k.astype(BF), joined[:, 2 * GROUP :].astype(BF)

    def put_q(p, half, q):
        row = p * 160 + half * 80
        none = jnp.zeros(q.shape, BF)
        qm[row : row + 80, :] = jnp.where(first, q, none)
        qm[640 + row : 720 + row, :] = jnp.where(first, none, q)

    def project_own(p):
        q, k, v = project(p, 1, w_ref)
        put_q(p, 0, q)
        kv[p, 0, 0, 0, 0:80] = k
        kv[p, 0, 0, 1, 0:80] = v

    def project_swap(p, n=1):
        q, k, v = project(p, n, wp)
        for i in range(n):
            rows = slice(i * 80, i * 80 + 80)
            swap[p + i, 0] = q[rows]
            swap[p + i, 1] = k[rows]
            swap[p + i, 2] = v[rows]
        for i in range(n):
            at = p + i
            link.send(
                ("kvswap", at),
                lambda at=at: swap.at[at, pl.ds(1, 2)],
                lambda at=at: kv.at[at, 0, 0, :, pl.ds(80, 80)],
                here.yhi,
            )
            link.send(("qswap", at), lambda at=at: swap.at[at, 0], lambda at=at: qin.at[at], here.yhi)

    def kv_from_y(p):
        link.wait(("kvswap", p), lambda: kv.at[p, 0, 0, :, pl.ds(80, 80)], here.yhi)

    def kv_at(p, x, j, kind=None):
        if kind is None:
            return lambda: kv.at[p, x, j]
        return lambda: kv.at[p, x, j, kind]

    def kv_send(p, src, dst, dev, kind=None):
        link.send(("kv", p, dst, kind), kv_at(p, *src, kind), kv_at(p, *dst, kind), dev)

    def kv_wait(p, dst, kind=None):
        link.wait(("kv", p, dst, kind), kv_at(p, *dst, kind), here.sib)

    def spread(p, y):
        kv_send(p, (0, y), (1, y), here.xp)
        kv_send(p, (0, y), (2, y), here.xm)
        kv_send(p, (0, y), (0, 2 + y), here.sib)

    def begin(p):
        kv_from_y(p)
        kv_send(p, (0, 0), (0, 1), here.ylo)
        spread(p, 0)

    def arrive_y(p):
        kv_wait(p, (0, 1))
        spread(p, 1)

    def relay(p, y):
        kv_wait(p, (1, y))
        kv_send(p, (1, y), (3, y), here.xp, 0)
        kv_send(p, (1, y), (1, 2 + y), here.sib)
        kv_wait(p, (2, y))
        kv_send(p, (2, y), (3, y), here.xm, 1)
        kv_send(p, (2, y), (2, 2 + y), here.sib)

    def finish(p, y):
        kv_wait(p, (3, y), 0)
        kv_wait(p, (3, y), 1)
        kv_send(p, (3, y), (3, 2 + y), here.sib)

    def from_sib(p, x):
        kv_wait(p, (x, 2))
        kv_wait(p, (x, 3))

    w_wait0 = lambda: wp.at[:, f]
    link.wait("w", w_wait0, here.yhi)
    w_send("ylo", f, here.ylo)
    w_spread(0)

    wait_tok(0)
    send_tok(1)
    for d in range(1, 16):
        peer = lax.rem(s + 16 - d, 16)
        link.wait(("mod", d), lambda: modbuf.at[peer], (f, peer))
    for i in range(8):
        low, high = modbuf[2 * i], modbuf[2 * i + 1]
        modt[9 * i : 9 * i + 4, :] = low[0:4]
        modt[9 * i + 4 : 9 * i + 5, :] = low[4:5] + high[0:1]
        modt[9 * i + 5 : 9 * i + 9, :] = high[1:5]
    modulate(1, 1, 2)
    w_wait("ylo", here.frame_at(1, 0, 0))
    w_spread(1)
    w_relay(0)
    project_own(1)

    wait_tok(1)
    send_tok(2)
    w_relay(1)
    modulate(2, 3, 4)
    w_finish(0)
    project_own(2)
    w_finish(1)

    wait_tok(2)
    link.send(("up", 3), lambda: blocks.at[5, 0], lambda: blocks.at[7, 0], here.zp)
    link.send(("down", 3), lambda: blocks.at[6, 1], lambda: blocks.at[7, 1], here.zm)
    wo_start()
    w_from_sib(0)
    w_from_sib(1)
    project_swap(1, 2)
    modulate(3, 5, 6)
    project_own(3)
    begin(1)
    project_swap(3)
    begin(2)
    link.wait(("up", 3), lambda: blocks.at[7, 0], here.zm)
    link.wait(("down", 3), lambda: blocks.at[7, 1], here.zp)
    modulate(0, 0, 7)
    project_swap(0)
    arrive_y(1)
    project_own(0)
    begin(3)
    relay(1, 0)
    arrive_y(2)
    begin(0)
    relay(1, 1)
    relay(2, 0)
    for p in range(4):
        link.wait(("qswap", p), lambda: qin.at[p], here.yhi)
        put_q(p, 1, qin[p])

    upper = lax.broadcasted_iota(jnp.int32, (GROUP, 640), 0) < HEAD

    def attend(t):
        p, x = (t // 4 + 1) % 4, t % 4
        keys = kv[p, x, :, 0].reshape(640, GROUP)
        values = kv[p, x, :, 1].reshape(640, GROUP).T
        one = jnp.ones((GROUP, 640), BF)
        vt[0] = jnp.where(upper, values, one)
        vt[1] = jnp.where(upper, one, values)
        for n in range(10):
            cols = slice(n * 128, (n + 1) * 128)
            scores = lax.dot_general(
                keys, qm[cols, :], (((1,), (1,)), ((), ())), preferred_element_type=F32
            )
            old = top[0:1, cols]
            new = jnp.maximum(old, jnp.max(scores, axis=0, keepdims=True))
            probs = jnp.exp2(scores - new).astype(BF)
            top[0:1, cols] = new
            part = jnp.dot(vt[n // 5], probs, preferred_element_type=F32)
            acc[:, cols] = acc[:, cols] * jnp.exp2(old - new) + part

    events = {
        0: [(arrive_y, 3), (finish, 1, 0)],
        1: [(relay, 2, 1), (finish, 1, 1), (wo_relay, 1, 0)],
        2: [(relay, 3, 0)],
        3: [(arrive_y, 0), (finish, 2, 0), (wo_relay, 1, 1)],
        4: [(finish, 2, 1), (relay, 3, 1)],
        5: [(relay, 0, 0)],
        6: [(finish, 3, 0), (wo_relay, 2, 0)],
        7: [(relay, 0, 1), (finish, 3, 1)],
        8: [(finish, 0, 0)],
        9: [(finish, 0, 1), (wo_relay, 2, 1)],
        11: [(wo_relay, 3, 0)],
        14: [(wo_relay, 3, 1)],
    }
    for t in range(16):
        events.setdefault(t, []).append((from_sib, (t // 4 + 1) % 4, t % 4))

    def step(t, carry):
        for when, acts in events.items():

            @pl.when(t == when)
            def _():
                for act, *args in acts:
                    act(*args)

        attend(t)
        return carry

    lax.fori_loop(0, 16, step, 0)

    upper_part = acc[0:64, 0:640] / acc[64:65, 0:640]
    lower_part = acc[64:128, 640:1280] / acc[0:1, 640:1280]
    mixed[...] = jnp.concatenate([upper_part, lower_part], axis=0).T

    def rows_of(p, b):
        base = p * 160 + b * 40
        return jnp.concatenate([mixed[base : base + 40], mixed[base + 80 : base + 120]], axis=0).astype(BF)

    targets = [(p, b) for p in (1, 2, 3) for b in (0, 1)] + [(0, 1)]
    for i, (p, b) in enumerate(targets):
        outbox[i] = rows_of(p, b)
        dev = here.along_z((4 if p == 0 else p) if b else -p)
        link.send(("mix", i), lambda i=i: outbox.at[i], lambda: lhs.at[z], dev)
    lhs[z] = rows_of(0, 0)
    wo_relay(4, 0)
    wo_relay(4, 1)
    for d in (1, 2, 3, 4):
        for h in range(2):
            wo_from_sib(d, h)
    for i, (p, b) in enumerate(targets):
        source = here.z_at((-4 if p == 0 else -p) if b else p)
        link.wait(("mix", i), lambda source=source: lhs.at[source], here.zp)

    for m in range(4):
        h, c = m // 2, (m % 2) * 768
        total = jnp.zeros((80, 768), F32)
        for i in range(4):
            left = jnp.concatenate([lhs[2 * i], lhs[2 * i + 1]], axis=1)
            right = wz[2 * i : 2 * i + 2, :, h, :, c : c + 768].reshape(256, 768)
            total = total + jnp.dot(left, right, preferred_element_type=F32)
        own_part[m] = total[:40]
        give[m] = jnp.concatenate([total[40:, :384], total[40:, 384:]], axis=0).astype(BF)
        link.send(("give", m), lambda m=m: give.at[m], lambda m=m: take_in.at[m], here.yhi)
    for m in range(4):
        link.wait(("give", m), lambda m=m: take_in.at[m], here.yhi)
        got = take_in[m].astype(F32)
        for half in range(2):
            for c in range(3):
                t = m * 6 + half * 3 + c
                cols = slice(c * 128, (c + 1) * 128)
                total = own_part[m, :, half * 384 + c * 128 : half * 384 + (c + 1) * 128]
                total = total + got[half * 40 : half * 40 + 40, cols]
                base = tok_ref[:, t * 128 : (t + 1) * 128].astype(F32)
                moved[half * 40 : half * 40 + 40, cols] = base + total * modt[48 + t : 49 + t, :]
        arrived[0, m] = moved[...].astype(BF)
        link.send(("shift", m), lambda m=m: arrived.at[0, m], lambda m=m: arrived.at[1, m], here.prev)
    last = f == 15
    fresh = fresh_ref[...].astype(F32)
    for m in range(4):
        link.wait(("shift", m), lambda m=m: arrived.at[1, m], here.next)
        got = arrived[1, m].astype(F32)
        for half in range(2):
            cols = slice(m * 768 + half * 384, m * 768 + (half + 1) * 384)
            out_ref[:, cols] = jnp.where(last, fresh[:, cols], got[half * 40 : half * 40 + 40]).astype(BF)
    link.drain()
    assert len(link.ids) <= N_COPIES, len(link.ids)


def layer_call(*operands):
    vm = pl.BlockSpec(memory_space=pltpu.VMEM)
    return pl.pallas_call(
        layer_kernel,
        out_shape=jax.ShapeDtypeStruct((TOK, D), BF),
        in_specs=[vm] * len(operands),
        out_specs=vm,
        scratch_shapes=[
            pltpu.VMEM((8, 2, 80, 768), BF),
            pltpu.VMEM((16, 8, 128), F32),
            pltpu.VMEM((72, 128), F32),
            pltpu.VMEM((3, 16, 192, GROUP), BF),
            pltpu.VMEM((4, 4, 80, 768), BF),
            pltpu.VMEM((4, 3, 80, GROUP), BF),
            pltpu.VMEM((4, 80, GROUP), BF),
            pltpu.VMEM((4, 4, 4, 2, 160, GROUP), BF),
            pltpu.VMEM((1280, GROUP), BF),
            pltpu.VMEM((2, GROUP, 640), BF),
            pltpu.VMEM((GROUP, 1280), F32),
            pltpu.VMEM((8, 1280), F32),
            pltpu.VMEM((8, 2, 2, 64, 1536), BF),
            pltpu.VMEM((640, GROUP), F32),
            pltpu.VMEM((7, 80, GROUP), BF),
            pltpu.VMEM((8, 80, GROUP), BF),
            pltpu.VMEM((4, 40, 768), F32),
            pltpu.VMEM((4, 80, 384), BF),
            pltpu.VMEM((4, 80, 384), BF),
            pltpu.VMEM((80, 384), F32),
            pltpu.VMEM((2, 4, 80, 384), BF),
            pltpu.SemaphoreType.DMA((N_COPIES,)),
            pltpu.SemaphoreType.DMA((N_COPIES,)),
        ],
        compiler_params=pltpu.CompilerParams(
            collective_id=0, has_side_effects=True, vmem_limit_bytes=VMEM_LIMIT
        ),
        name="layer",
    )(*operands)


def body(queue_tokens, timesteps, fresh_noise, w_mod, w_qkv, q_gain, k_gain, w_out):
    condition = jax.nn.silu(embed_steps(timesteps)).astype(BF)
    own = jnp.dot(condition, w_mod, preferred_element_type=F32)
    even = lax.axis_index("seq") % 2 == 0
    mod = jnp.where(even, jnp.pad(own, ((0, 0), (0, 64))), jnp.pad(own, ((0, 0), (64, 0))))
    mod = jnp.pad(mod.reshape(5, 128), ((0, 3), (0, 0)))
    w = jnp.transpose(w_qkv, (1, 0, 2)).reshape(3, 16, 192, GROUP)
    qg = jnp.concatenate([q_gain, q_gain])[None]
    kg = jnp.concatenate([k_gain, k_gain])[None]
    return layer_call(queue_tokens[0], mod, w, w_out, qg, kg, fresh_noise)[None]


def solution(mesh):
    return jax.shard_map(
        body,
        mesh=mesh,
        in_specs=(
            P("frame", "seq", None),
            P("frame"),
            P("seq", None),
            P(None, "seq"),
            P(None, None, "seq"),
            P(),
            P(),
            P("seq", None),
        ),
        out_specs=P("frame", "seq", None),
        check_vma=False,
    )
```

time: 523 us -> 108 us (0.21)
  waiting for transfers between devices: 355 us -> 0 us
  Pallas kernels: 0 us -> 103 us
  blocking collectives: 66.8 us -> 0 us
  matrix products: 35.3 us -> 0.25 us
  local copies, waits for them, and re-layouts: 27 us -> 2.26 us
  other arithmetic: 15.6 us -> 1.55 us
  between operations: 14.7 us -> 0.76 us
  starting transfers between devices: 7.09 us -> 0 us
    reduce_scatter x1 -> x0, waiting for transfers between devices: 208 us -> none  [body(): lax.psum_scatter(lax.optimization_barrier(term.astype(jnp.bfloat16)).asty...]
    all_gather x2 -> x0, waiting for transfers between devices: 142 us -> none  [the longest x1 101 us: body(): shard_rows = lax.all_gather(modded, 'seq', axis=0, tiled=True)]
    pallas_call x0 -> x1, Pallas kernels: none -> 103 us  [layer_call(): pl.pallas_call(layer_kernel, out_shape=jax.ShapeDtypeStruct((TOK, D), BF)...]
    unnamed x1 -> x0, blocking collectives: 66.8 us -> none
    dot_general x13 -> x1, matrix products: 35.3 us -> 0.25 us  [body(): own = jnp.dot(condition, w_mod, preferred_element_type=F32)]
    reduce_sum x9 -> x0, other arithmetic: 11.7 us -> none  [the longest x5 9.28 us: one_block(): summed = jnp.sum(exponent, axis=(2, 3), keepdims=True)]
    slice x5 -> x0, local copies, waits for them, and re-layouts: 11.5 us -> none  [the longest x2 8.92 us: body(): every_frame[:, :, group_width:]]
    ppermute x1 -> x0, starting transfers between devices: 7 us -> none  [shifted(): return lax.ppermute(value, axis, pairs)]
  transfers between devices with their start and end apart: 4 -> 0, of which waited for: 4 -> 0; matrix products, arithmetic and copies ran while one was open for 1% -> 0% of each run, Pallas kernels for 0% -> 0%
where the time goes in v3:
time: 108 us
  Pallas kernels  103 us (95%)
  local copies, waits for them, and re-layouts  2.26 us (2%)
  other arithmetic  1.55 us (1%)
    pallas_call x1, Pallas kernels, layer_call(): pl.pallas_call(layer_kernel, out_shape=jax.ShapeDtypeStruct((TOK, D), BF)...  103 us

profile of v3, /device:TPU:1, one launch (start us, length us, event | category | flops | bytes accessed | tf_op | source)
XLA Modules:
  0.0 107.7 jit_solution(7875976261186166380)
XLA Ops:
  0.0 0.0 copy-start
  0.7 1.4 %maximum_bitcast_fusion = (f32[1,128]{1,0:T(1,128)}, f32[1,128]{1,0:T(1,128)}) fusion(f32[64]{0:T(128)} %param.13, f32[64]{0:T(128)} %param.14), kind=kLoop, calls=%fused_computation.8 | loop fusion | flops 256 | bytes 1536 | tf_op jit(solution)/shard_map/broadcast_in_dim | solution.py:555
  2.2 0.0 copy-done
  2.2 0.2 fusion.4
  2.4 0.1 fusion
  2.6 0.6 pad.14.mod_ref
  3.2 102.9 %layer.1 = bf16[40,3072]{1,0:T(8,128)(2,1)} custom-call(bf16[40,3072]{1,0:T(8,128)(2,1)} %bitcast.15, f32[8,128]{1,0:T(8,128)} %pad.14.mod_ref, bf16[3,16,192,128]{3,2,1,0:T(8,128)(2,1)} %bitcast.13, bf16[128,3072]{1,0:T(8,128)(2,1)} %wo_ref.1, f32[1,128]{1,0:T(1,128)} %get-tuple-element.7.qg_ref, f32[1,128]{1,0:T(1,128)} %get-tuple-element.8.kg_ref, ...), custom_call_target="tpu_custom_call" | custom-call | tf_op jit(solution)/shard_map/layer/pallas_call | solution.py:511
  106.0 1.7 %copy.11 = bf16[1,40,3072]{2,1,0:T(8,128)(2,1)} copy(bf16[1,40,3072]{2,1,0:T(8,128)(2,1)} %bitcast.14) | data formatting | bytes 491520
  (3 shorter events, 0.1 us)
Async XLA Ops:
  0.0 2.2 %copy-start = (bf16[512,576]{0,1:T(8,128)(2,1)S(1)}, bf16[512,576]{0,1:T(8,128)(2,1)}, u32[]{:S(2)}) copy-start(bf16[512,576]{0,1:T(8,128)(2,1)} %param.11) | copy-start | bytes 1769476

commit v4 on v3

--- a/solution.py
+++ b/solution.py
@@ -84,6 +84,7 @@
     def drain(self):
         for sent in self.sent:
             self._copy(*sent).wait_send()
+        self.sent = []
 
 
 def meet(devices):
@@ -116,11 +117,11 @@
 
 
 def layer_kernel(
-    tok_ref, mod_ref, w_ref, wo_ref, qg_ref, kg_ref, fresh_ref,
+    tok_ref, cond_ref, wm_hbm, w_hbm, wo_hbm, qg_ref, kg_ref,
     out_ref,
-    blocks, modbuf, modt, wp, x_scr, swap, qin, kv, qm, vt, acc, top,
+    wm_ref, w_ref, blocks, modbuf, modt, wp, x_scr, swap, qin, kv, qm, vt, acc, top,
     wz, mixed, outbox, lhs, own_part, give, take_in, moved, arrived,
-    send_sem, recv_sem,
+    joined, send_sem, recv_sem, local_sem,
 ):
     here = Place()
     f, s, z, core = here.f, here.s, here.z, here.core
@@ -128,19 +129,35 @@
     ready = meet(seq_peers + [here.sib, here.ylo, here.xp, here.xm, here.far])
     link = Link(send_sem, recv_sem)
 
+    local = [
+        pltpu.make_async_copy(wm_hbm, wm_ref, local_sem.at[0]),
+        pltpu.make_async_copy(w_hbm, w_ref, local_sem.at[1]),
+    ]
+    for c in range(2):
+        for h in range(2):
+            src = wo_hbm.at[pl.ds(c * 64, 64), pl.ds(h * 1536, 1536)]
+            local.append(pltpu.make_async_copy(src, wz.at[z, c, h], local_sem.at[2 + 2 * c + h]))
+    for copy in local:
+        copy.start()
     tok = tok_ref[...].astype(F32)
     for h, piece in enumerate(to_block(tok)):
         blocks[0, h] = piece.astype(BF)
-    modbuf[s] = mod_ref[...]
-    for c in range(2):
-        for h in range(2):
-            wz[z, c, h] = wo_ref[c * 64 : (c + 1) * 64, h * 1536 : (h + 1) * 1536]
+    local[0].wait()
+    own = lax.dot_general(
+        jnp.broadcast_to(cond_ref[...].astype(F32), (16, TEMB)).astype(BF), wm_ref[...], (((1,), (1,)), ((), ())), preferred_element_type=F32
+    )[0:1]
+    gap = jnp.zeros((1, 64), F32)
+    even = jnp.concatenate([own, gap], axis=1)
+    odd = jnp.concatenate([gap, own], axis=1)
+    own = jnp.where(s % 2 == 0, even, odd)
+    modbuf[s] = jnp.zeros((8, 128), F32)
+    for i in range(5):
+        modbuf[s, i : i + 1, :] = own[:, i * 128 : (i + 1) * 128]
     acc[...] = jnp.zeros(acc.shape, F32)
     top[...] = jnp.full(top.shape, -1e30, F32)
     ready()
 
-    for d, dev in enumerate(seq_peers):
-        link.send(("mod", d + 1), lambda: modbuf.at[s], lambda: modbuf.at[s], dev)
+    link.send("w", lambda: w_hbm.at[:, f], lambda: wp.at[:, f], here.yhi)
 
     def send_tok(j):
         src = (0, 1, 3)[j], (0, 2, 4)[j]
@@ -154,7 +171,8 @@
         link.wait(("down", j), lambda: blocks.at[dst[1]], here.zp)
 
     send_tok(0)
-    link.send("w", lambda: w_ref.at[:, f], lambda: wp.at[:, f], here.yhi)
+    for d, dev in enumerate(seq_peers):
+        link.send(("mod", d + 1), lambda: modbuf.at[s], lambda: modbuf.at[s], dev)
 
     def slice_of(who, half=None):
         if half is None:
@@ -198,7 +216,7 @@
     def wo_start():
         rows = pl.ds(pl.multiple_of(core * 64, 64), 64)
         for h in range(2):
-            src = lambda h=h: wo_ref.at[rows, pl.ds(h * 1536, 1536)]
+            src = lambda h=h: wo_hbm.at[rows, pl.ds(h * 1536, 1536)]
             link.send(("wo", "up", 1, h), src, wo_at(z, core, h), here.zp)
             link.send(("wo", "down", 1, h), src, wo_at(z, core, h), here.zm)
 
@@ -253,18 +271,28 @@
                     out = both * scale + modt[t : t + 1, :]
                     x_scr[p, t // 6, :, (t % 6) * 128 : (t % 6 + 1) * 128] = out.astype(BF)
 
-    def project(p, n, weights):
-        def step(k, total):
-            part = jnp.concatenate(
-                [weights[j, pl.ds(k * 4, 4)].reshape(768, GROUP) for j in range(3)], axis=1
+    q_gain = jnp.concatenate([qg_ref[...]] * 2, axis=1) * q_scale
+    k_gain = jnp.concatenate([kg_ref[...]] * 2, axis=1)
+
+    def finish_qkv(qkv):
+        q = head_norm_pair(qkv[:, :GROUP], q_gain, first)
+        k = head_norm_pair(qkv[:, GROUP : 2 * GROUP], k_gain, first)
+        return q.astype(BF), k.astype(BF), qkv[:, 2 * GROUP :].astype(BF)
+
+    def project(p, n=1):
+        rows = n * 80
+        x = jnp.concatenate([x_scr[p : p + n, k].reshape(rows, 768) for k in range(4)], axis=1)
+        sides = [side[j] for side in (wp, w_ref) for j in range(3)]
+        for pair in range(3):
+            part = jnp.concatenate([sides[2 * pair + i].reshape(D, GROUP) for i in range(2)], axis=1)
+            joined[0:rows, pair * 256 : (pair + 1) * 256] = jnp.dot(
+                x, part, preferred_element_type=F32
             )
-            rows = x_scr[p : p + n, k].reshape(n * 80, 768)
-            return total + jnp.dot(rows, part, preferred_element_type=F32)
-
-        joined = lax.fori_loop(0, 4, step, jnp.zeros((n * 80, 3 * GROUP), F32))
-        q = head_norm_pair(joined[:, :GROUP], qg_ref[...], first) * q_scale
-        k = head_norm_pair(joined[:, GROUP : 2 * GROUP], kg_ref[...], first)
-        return q.astype(BF), k.astype(BF), joined[:, 2 * GROUP :].astype(BF)
+        for i in range(n):
+            keep_swap(p + i, *finish_qkv(joined[i * 80 : i * 80 + 80, : 3 * GROUP]))
+            send_swap(p + i)
+        for i in range(n):
+            keep_own(p + i, *finish_qkv(joined[i * 80 : i * 80 + 80, 3 * GROUP :]))
 
     def put_q(p, half, q):
         row = p * 160 + half * 80
@@ -272,28 +300,24 @@
         qm[row : row + 80, :] = jnp.where(first, q, none)
         qm[640 + row : 720 + row, :] = jnp.where(first, none, q)
 
-    def project_own(p):
-        q, k, v = project(p, 1, w_ref)
+    def keep_own(p, q, k, v):
         put_q(p, 0, q)
         kv[p, 0, 0, 0, 0:80] = k
         kv[p, 0, 0, 1, 0:80] = v
 
-    def project_swap(p, n=1):
-        q, k, v = project(p, n, wp)
-        for i in range(n):
-            rows = slice(i * 80, i * 80 + 80)
-            swap[p + i, 0] = q[rows]
-            swap[p + i, 1] = k[rows]
-            swap[p + i, 2] = v[rows]
-        for i in range(n):
-            at = p + i
-            link.send(
-                ("kvswap", at),
-                lambda at=at: swap.at[at, pl.ds(1, 2)],
-                lambda at=at: kv.at[at, 0, 0, :, pl.ds(80, 80)],
-                here.yhi,
-            )
-            link.send(("qswap", at), lambda at=at: swap.at[at, 0], lambda at=at: qin.at[at], here.yhi)
+    def keep_swap(p, q, k, v):
+        swap[p, 0] = q
+        swap[p, 1] = k
+        swap[p, 2] = v
+
+    def send_swap(p):
+        link.send(
+            ("kvswap", p),
+            lambda: swap.at[p, pl.ds(1, 2)],
+            lambda: kv.at[p, 0, 0, :, pl.ds(80, 80)],
+            here.yhi,
+        )
+        link.send(("qswap", p), lambda: swap.at[p, 0], lambda: qin.at[p], here.yhi)
 
     def kv_from_y(p):
         link.wait(("kvswap", p), lambda: kv.at[p, 0, 0, :, pl.ds(80, 80)], here.yhi)
@@ -309,10 +333,16 @@
     def kv_wait(p, dst, kind=None):
         link.wait(("kv", p, dst, kind), kv_at(p, *dst, kind), here.sib)
 
+    def to_sib(p, x):
+        src, dst = (lambda: kv.at[p, x, pl.ds(0, 2)]), (lambda: kv.at[p, x, pl.ds(2, 2)])
+        link.send(("sib", p, x), src, dst, here.sib)
+
+    def from_sib(p, x):
+        link.wait(("sib", p, x), lambda: kv.at[p, x, pl.ds(2, 2)], here.sib)
+
     def spread(p, y):
         kv_send(p, (0, y), (1, y), here.xp)
         kv_send(p, (0, y), (2, y), here.xm)
-        kv_send(p, (0, y), (0, 2 + y), here.sib)
 
     def begin(p):
         kv_from_y(p)
@@ -322,23 +352,22 @@
     def arrive_y(p):
         kv_wait(p, (0, 1))
         spread(p, 1)
+        to_sib(p, 0)
 
     def relay(p, y):
         kv_wait(p, (1, y))
         kv_send(p, (1, y), (3, y), here.xp, 0)
-        kv_send(p, (1, y), (1, 2 + y), here.sib)
         kv_wait(p, (2, y))
         kv_send(p, (2, y), (3, y), here.xm, 1)
-        kv_send(p, (2, y), (2, 2 + y), here.sib)
-
-    def finish(p, y):
-        kv_wait(p, (3, y), 0)
-        kv_wait(p, (3, y), 1)
-        kv_send(p, (3, y), (3, 2 + y), here.sib)
-
-    def from_sib(p, x):
-        kv_wait(p, (x, 2))
-        kv_wait(p, (x, 3))
+        if y == 1:
+            to_sib(p, 1)
+            to_sib(p, 2)
+
+    def finish(p):
+        for y in range(2):
+            kv_wait(p, (3, y), 0)
+            kv_wait(p, (3, y), 1)
+        to_sib(p, 3)
 
     w_wait0 = lambda: wp.at[:, f]
     link.wait("w", w_wait0, here.yhi)
@@ -347,6 +376,9 @@
 
     wait_tok(0)
     send_tok(1)
+    w_wait("ylo", here.frame_at(1, 0, 0))
+    w_spread(1)
+    w_relay(0)
     for d in range(1, 16):
         peer = lax.rem(s + 16 - d, 16)
         link.wait(("mod", d), lambda: modbuf.at[peer], (f, peer))
@@ -356,46 +388,36 @@
         modt[9 * i + 4 : 9 * i + 5, :] = low[4:5] + high[0:1]
         modt[9 * i + 5 : 9 * i + 9, :] = high[1:5]
     modulate(1, 1, 2)
-    w_wait("ylo", here.frame_at(1, 0, 0))
-    w_spread(1)
-    w_relay(0)
-    project_own(1)
+    w_finish(0)
+    local[1].wait()
 
     wait_tok(1)
     send_tok(2)
     w_relay(1)
     modulate(2, 3, 4)
-    w_finish(0)
-    project_own(2)
     w_finish(1)
+    w_from_sib(0)
+    w_from_sib(1)
+    project(1, 2)
 
     wait_tok(2)
     link.send(("up", 3), lambda: blocks.at[5, 0], lambda: blocks.at[7, 0], here.zp)
     link.send(("down", 3), lambda: blocks.at[6, 1], lambda: blocks.at[7, 1], here.zm)
-    wo_start()
-    w_from_sib(0)
-    w_from_sib(1)
-    project_swap(1, 2)
+    begin(1)
+    begin(2)
     modulate(3, 5, 6)
-    project_own(3)
-    begin(1)
-    project_swap(3)
-    begin(2)
+    project(3)
     link.wait(("up", 3), lambda: blocks.at[7, 0], here.zm)
     link.wait(("down", 3), lambda: blocks.at[7, 1], here.zp)
+    wo_start()
+    arrive_y(1)
     modulate(0, 0, 7)
-    project_swap(0)
-    arrive_y(1)
-    project_own(0)
+    project(0)
     begin(3)
-    relay(1, 0)
-    arrive_y(2)
+    for p in (1, 2, 3, 0):
+        link.wait(("qswap", p), lambda p=p: qin.at[p], here.yhi)
+        put_q(p, 1, qin[p])
     begin(0)
-    relay(1, 1)
-    relay(2, 0)
-    for p in range(4):
-        link.wait(("qswap", p), lambda: qin.at[p], here.yhi)
-        put_q(p, 1, qin[p])
 
     upper = lax.broadcasted_iota(jnp.int32, (GROUP, 640), 0) < HEAD
 
@@ -419,18 +441,19 @@
             acc[:, cols] = acc[:, cols] * jnp.exp2(old - new) + part
 
     events = {
-        0: [(arrive_y, 3), (finish, 1, 0)],
-        1: [(relay, 2, 1), (finish, 1, 1), (wo_relay, 1, 0)],
-        2: [(relay, 3, 0)],
-        3: [(arrive_y, 0), (finish, 2, 0), (wo_relay, 1, 1)],
-        4: [(finish, 2, 1), (relay, 3, 1)],
-        5: [(relay, 0, 0)],
-        6: [(finish, 3, 0), (wo_relay, 2, 0)],
-        7: [(relay, 0, 1), (finish, 3, 1)],
-        8: [(finish, 0, 0)],
-        9: [(finish, 0, 1), (wo_relay, 2, 1)],
-        11: [(wo_relay, 3, 0)],
-        14: [(wo_relay, 3, 1)],
+        0: [(arrive_y, 2), (relay, 1, 0), (relay, 1, 1), (wo_relay, 1, 0)],
+        1: [(relay, 2, 0), (wo_relay, 1, 1)],
+        2: [(arrive_y, 3), (finish, 1)],
+        3: [(relay, 2, 1)],
+        4: [(arrive_y, 0), (relay, 3, 0), (wo_relay, 2, 0)],
+        5: [(finish, 2), (relay, 3, 1)],
+        6: [(relay, 0, 0), (wo_relay, 2, 1)],
+        7: [(relay, 0, 1)],
+        8: [(finish, 3)],
+        9: [(wo_relay, 3, 0)],
+        10: [(finish, 0)],
+        12: [(wo_relay, 3, 1)],
+        15: [(wo_relay, 4, 0), (wo_relay, 4, 1)],
     }
     for t in range(16):
         events.setdefault(t, []).append((from_sib, (t // 4 + 1) % 4, t % 4))
@@ -462,8 +485,7 @@
         dev = here.along_z((4 if p == 0 else p) if b else -p)
         link.send(("mix", i), lambda i=i: outbox.at[i], lambda: lhs.at[z], dev)
     lhs[z] = rows_of(0, 0)
-    wo_relay(4, 0)
-    wo_relay(4, 1)
+    link.drain()
     for d in (1, 2, 3, 4):
         for h in range(2):
             wo_from_sib(d, h)
@@ -471,13 +493,14 @@
         source = here.z_at((-4 if p == 0 else -p) if b else p)
         link.wait(("mix", i), lambda source=source: lhs.at[source], here.zp)
 
+    for copy in local[2:]:
+        copy.wait()
+
+    left = jnp.concatenate([lhs[i] for i in range(8)], axis=1)
     for m in range(4):
         h, c = m // 2, (m % 2) * 768
-        total = jnp.zeros((80, 768), F32)
-        for i in range(4):
-            left = jnp.concatenate([lhs[2 * i], lhs[2 * i + 1]], axis=1)
-            right = wz[2 * i : 2 * i + 2, :, h, :, c : c + 768].reshape(256, 768)
-            total = total + jnp.dot(left, right, preferred_element_type=F32)
+        right = wz[:, :, h, :, c : c + 768].reshape(1024, 768)
+        total = jnp.dot(left, right, preferred_element_type=F32)
         own_part[m] = total[:40]
         give[m] = jnp.concatenate([total[40:, :384], total[40:, 384:]], axis=0).astype(BF)
         link.send(("give", m), lambda m=m: give.at[m], lambda m=m: take_in.at[m], here.yhi)
@@ -494,26 +517,26 @@
                 moved[half * 40 : half * 40 + 40, cols] = base + total * modt[48 + t : 49 + t, :]
         arrived[0, m] = moved[...].astype(BF)
         link.send(("shift", m), lambda m=m: arrived.at[0, m], lambda m=m: arrived.at[1, m], here.prev)
-    last = f == 15
-    fresh = fresh_ref[...].astype(F32)
     for m in range(4):
         link.wait(("shift", m), lambda m=m: arrived.at[1, m], here.next)
-        got = arrived[1, m].astype(F32)
         for half in range(2):
             cols = slice(m * 768 + half * 384, m * 768 + (half + 1) * 384)
-            out_ref[:, cols] = jnp.where(last, fresh[:, cols], got[half * 40 : half * 40 + 40]).astype(BF)
+            out_ref[:, cols] = arrived[1, m].astype(F32)[half * 40 : half * 40 + 40].astype(BF)
     link.drain()
     assert len(link.ids) <= N_COPIES, len(link.ids)
 
 
 def layer_call(*operands):
     vm = pl.BlockSpec(memory_space=pltpu.VMEM)
+    hbm = pl.BlockSpec(memory_space=pl.ANY)
     return pl.pallas_call(
         layer_kernel,
         out_shape=jax.ShapeDtypeStruct((TOK, D), BF),
-        in_specs=[vm] * len(operands),
+        in_specs=[vm, vm, hbm, hbm, hbm, vm, vm],
         out_specs=vm,
         scratch_shapes=[
+            pltpu.VMEM((576, TEMB), BF),
+            pltpu.VMEM((3, 16, 192, GROUP), BF),
             pltpu.VMEM((8, 2, 80, 768), BF),
             pltpu.VMEM((16, 8, 128), F32),
             pltpu.VMEM((72, 128), F32),
@@ -535,8 +558,10 @@
             pltpu.VMEM((4, 80, 384), BF),
             pltpu.VMEM((80, 384), F32),
             pltpu.VMEM((2, 4, 80, 384), BF),
+            pltpu.VMEM((160, 6 * GROUP), F32),
             pltpu.SemaphoreType.DMA((N_COPIES,)),
             pltpu.SemaphoreType.DMA((N_COPIES,)),
+            pltpu.SemaphoreType.DMA((6,)),
         ],
         compiler_params=pltpu.CompilerParams(
             collective_id=0, has_side_effects=True, vmem_limit_bytes=VMEM_LIMIT
@@ -547,14 +572,10 @@
 
 def body(queue_tokens, timesteps, fresh_noise, w_mod, w_qkv, q_gain, k_gain, w_out):
     condition = jax.nn.silu(embed_steps(timesteps)).astype(BF)
-    own = jnp.dot(condition, w_mod, preferred_element_type=F32)
-    even = lax.axis_index("seq") % 2 == 0
-    mod = jnp.where(even, jnp.pad(own, ((0, 0), (0, 64))), jnp.pad(own, ((0, 0), (64, 0))))
-    mod = jnp.pad(mod.reshape(5, 128), ((0, 3), (0, 0)))
     w = jnp.transpose(w_qkv, (1, 0, 2)).reshape(3, 16, 192, GROUP)
-    qg = jnp.concatenate([q_gain, q_gain])[None]
-    kg = jnp.concatenate([k_gain, k_gain])[None]
-    return layer_call(queue_tokens[0], mod, w, w_out, qg, kg, fresh_noise)[None]
+    arrived = layer_call(queue_tokens[0], condition, w_mod.T, w, w_out, q_gain[None], k_gain[None])
+    last = lax.axis_index("frame") == lax.axis_size("frame") - 1
+    return jnp.where(last, fresh_noise, arrived)[None]
 
 
 def solution(mesh):

time: 108 us -> 101 us (0.935)
  Pallas kernels: 103 us -> 97 us
  local copies, waits for them, and re-layouts: 2.26 us -> 0.01 us
    pallas_call x1, Pallas kernels: 103 us -> 97 us  [layer_call(): pl.pallas_call(layer_kernel, out_shape=jax.ShapeDtypeStruct((TOK, D), BF)...]
    unnamed x3 -> x2, local copies, waits for them, and re-layouts: 1.66 us -> 0.01 us
where the time goes in v4:
time: 101 us; the launch traced here: 100 us
  Pallas kernels  97 us (96%)
  other arithmetic  2.33 us (2%)
    pallas_call x1, Pallas kernels, layer_call(): pl.pallas_call(layer_kernel, out_shape=jax.ShapeDtypeStruct((TOK, D), BF)...  97 us

profile of v4, /device:TPU:1, one launch (start us, length us, event | category | flops | bytes accessed | tf_op | source)
XLA Modules:
  0.0 100.0 jit_solution(4420278519821928004)
XLA Ops:
  0.0 0.0 copy-start
  0.8 0.6 fusion.cond_ref
  1.4 97.0 %layer.1 = bf16[40,3072]{1,0:T(8,128)(2,1)} custom-call(bf16[40,3072]{1,0:T(8,128)(2,1)} %bitcast.14, bf16[1,512]{1,0:T(2,128)(2,1)} %fusion.cond_ref, bf16[576,512]{1,0:T(8,128)(2,1)} %bitcast.13, bf16[3,16,192,128]{3,2,1,0:T(8,128)(2,1)} %bitcast.12, bf16[128,3072]{1,0:T(8,128)(2,1)} %wo_hbm.1, f32[1,64]{1,0:T(1,128)} %bitcast.17, f32[1,64]{1,0:T(1,128)} %bitcast.18), custom_call_target="tpu_custom_call" | custom-call | tf_op jit(solution)/shard_map/layer/pallas_call | solution.py:532
  98.3 0.0 copy-done
  98.4 1.7 %select_bitcast_fusion = bf16[1,40,3072]{2,1,0:T(8,128)(2,1)} fusion(bf16[40,3072]{1,0:T(8,128)(2,1)S(1)} %copy-done, bf16[40,3072]{1,0:T(8,128)(2,1)} %layer.1, pred[]{:T(512)S(6)} %eq.3), kind=kLoop, calls=%fused_computation | loop fusion | flops 122880 | bytes 737281 | tf_op jit(solution)/shard_map/broadcast_in_dim | solution.py:578
  (1 shorter events, 0.0 us)
Async XLA Ops:
  0.0 98.3 %copy-start = (bf16[40,3072]{1,0:T(8,128)(2,1)S(1)}, bf16[40,3072]{1,0:T(8,128)(2,1)}, u32[]{:S(2)}) copy-start(bf16[40,3072]{1,0:T(8,128)(2,1)} %param.10) | copy-start | bytes 737284

commit v5 on v4

--- a/solution.py
+++ b/solution.py
@@ -44,6 +44,8 @@
         self.yhi = (f, (1 - yhi) * 8 + z)
         self.prev = ((f + 15) % 16, s)
         self.next = ((f + 1) % 16, s)
+        self.prev_y = ((f + 15) % 16, self.yhi[1])
+        self.next_y = ((f + 1) % 16, self.yhi[1])
         self.far = ((f + 15 + 2 * core) % 16, s)
 
     def frame_at(self, dy, dx, dc):
@@ -120,13 +122,13 @@
     tok_ref, cond_ref, wm_hbm, w_hbm, wo_hbm, qg_ref, kg_ref,
     out_ref,
     wm_ref, w_ref, blocks, modbuf, modt, wp, x_scr, swap, qin, kv, qm, vt, acc, top,
-    wz, mixed, outbox, lhs, own_part, give, take_in, moved, arrived,
+    wz, mixed, outbox, lhs, give, give_in, keep, keep_in, nexttok, nextgate, s_scr, p_scr,
     joined, send_sem, recv_sem, local_sem,
 ):
     here = Place()
     f, s, z, core = here.f, here.s, here.z, here.core
     seq_peers = [(f, lax.rem(s + d, 16)) for d in range(1, 16)]
-    ready = meet(seq_peers + [here.sib, here.ylo, here.xp, here.xm, here.far])
+    ready = meet(seq_peers + [here.sib, here.ylo, here.xp, here.xm, here.far, here.prev_y, here.next_y])
     link = Link(send_sem, recv_sem)
 
     local = [
@@ -428,17 +430,39 @@
         one = jnp.ones((GROUP, 640), BF)
         vt[0] = jnp.where(upper, values, one)
         vt[1] = jnp.where(upper, one, values)
+        def score(n):
+            s_scr[n % 2] = lax.dot_general(
+                keys, qm[n * 128 : (n + 1) * 128, :], (((1,), (1,)), ((), ())),
+                preferred_element_type=F32,
+            )
+
+        def weigh(n):
+            cols = slice(n * 128, (n + 1) * 128)
+            old = top[0:1, cols]
+            new = jnp.maximum(old, jnp.max(s_scr[n % 2], axis=0, keepdims=True))
+            p_scr[n % 2] = jnp.exp2(s_scr[n % 2] - new).astype(BF)
+            top[0:1, cols] = new
+            return jnp.exp2(old - new)
+
+        def mix(n, shrink):
+            cols = slice(n * 128, (n + 1) * 128)
+            part = jnp.dot(vt[n // 5], p_scr[n % 2], preferred_element_type=F32)
+            acc[:, cols] = acc[:, cols] * shrink + part
+
+        score(0)
+        shrink = None
         for n in range(10):
-            cols = slice(n * 128, (n + 1) * 128)
-            scores = lax.dot_general(
-                keys, qm[cols, :], (((1,), (1,)), ((), ())), preferred_element_type=F32
-            )
-            old = top[0:1, cols]
-            new = jnp.maximum(old, jnp.max(scores, axis=0, keepdims=True))
-            probs = jnp.exp2(scores - new).astype(BF)
-            top[0:1, cols] = new
-            part = jnp.dot(vt[n // 5], probs, preferred_element_type=F32)
-            acc[:, cols] = acc[:, cols] * jnp.exp2(old - new) + part
+            if n < 9:
+                score(n + 1)
+            now = weigh(n)
+            if n:
+                mix(n - 1, shrink)
+            shrink = now
+        mix(9, shrink)
+
+    def send_base():
+        link.send("tok", lambda: blocks.at[0], lambda: nexttok, here.prev)
+        link.send("gate", lambda: modt.at[pl.ds(48, 24)], lambda: nextgate, here.prev)
 
     events = {
         0: [(arrive_y, 2), (relay, 1, 0), (relay, 1, 1), (wo_relay, 1, 0)],
@@ -453,6 +477,7 @@
         9: [(wo_relay, 3, 0)],
         10: [(finish, 0)],
         12: [(wo_relay, 3, 1)],
+        13: [(send_base,)],
         15: [(wo_relay, 4, 0), (wo_relay, 4, 1)],
     }
     for t in range(16):
@@ -479,7 +504,7 @@
         base = p * 160 + b * 40
         return jnp.concatenate([mixed[base : base + 40], mixed[base + 80 : base + 120]], axis=0).astype(BF)
 
-    targets = [(p, b) for p in (1, 2, 3) for b in (0, 1)] + [(0, 1)]
+    targets = [(0, 1)] + [(p, b) for p in (3, 2, 1) for b in (0, 1)]
     for i, (p, b) in enumerate(targets):
         outbox[i] = rows_of(p, b)
         dev = here.along_z((4 if p == 0 else p) if b else -p)
@@ -501,27 +526,24 @@
         h, c = m // 2, (m % 2) * 768
         right = wz[:, :, h, :, c : c + 768].reshape(1024, 768)
         total = jnp.dot(left, right, preferred_element_type=F32)
-        own_part[m] = total[:40]
         give[m] = jnp.concatenate([total[40:, :384], total[40:, 384:]], axis=0).astype(BF)
-        link.send(("give", m), lambda m=m: give.at[m], lambda m=m: take_in.at[m], here.yhi)
+        link.send(("give", m), lambda m=m: give.at[m], lambda m=m: give_in.at[m], here.prev_y)
+        keep[m] = jnp.concatenate([total[:40, :384], total[:40, 384:]], axis=0).astype(BF)
+        link.send(("keep", m), lambda m=m: keep.at[m], lambda m=m: keep_in.at[m], here.prev)
+    link.wait("tok", lambda: nexttok, here.next)
+    link.wait("gate", lambda: nextgate, here.next)
     for m in range(4):
-        link.wait(("give", m), lambda m=m: take_in.at[m], here.yhi)
-        got = take_in[m].astype(F32)
+        h, k = m // 2, m % 2
+        base = nexttok[h].astype(F32)[k * 40 : k * 40 + 40]
+        link.wait(("keep", m), lambda m=m: keep_in.at[m], here.next)
+        link.wait(("give", m), lambda m=m: give_in.at[m], here.next_y)
+        total = keep_in[m].astype(F32) + give_in[m].astype(F32)
         for half in range(2):
             for c in range(3):
                 t = m * 6 + half * 3 + c
-                cols = slice(c * 128, (c + 1) * 128)
-                total = own_part[m, :, half * 384 + c * 128 : half * 384 + (c + 1) * 128]
-                total = total + got[half * 40 : half * 40 + 40, cols]
-                base = tok_ref[:, t * 128 : (t + 1) * 128].astype(F32)
-                moved[half * 40 : half * 40 + 40, cols] = base + total * modt[48 + t : 49 + t, :]
-        arrived[0, m] = moved[...].astype(BF)
-        link.send(("shift", m), lambda m=m: arrived.at[0, m], lambda m=m: arrived.at[1, m], here.prev)
-    for m in range(4):
-        link.wait(("shift", m), lambda m=m: arrived.at[1, m], here.next)
-        for half in range(2):
-            cols = slice(m * 768 + half * 384, m * 768 + (half + 1) * 384)
-            out_ref[:, cols] = arrived[1, m].astype(F32)[half * 40 : half * 40 + 40].astype(BF)
+                term = total[half * 40 : half * 40 + 40, c * 128 : (c + 1) * 128] * nextgate[t : t + 1, :]
+                at = half * 384 + c * 128
+                out_ref[:, t * 128 : (t + 1) * 128] = (base[:, at : at + 128] + term).astype(BF)
     link.drain()
     assert len(link.ids) <= N_COPIES, len(link.ids)
 
@@ -553,11 +575,14 @@
             pltpu.VMEM((640, GROUP), F32),
             pltpu.VMEM((7, 80, GROUP), BF),
             pltpu.VMEM((8, 80, GROUP), BF),
-            pltpu.VMEM((4, 40, 768), F32),
             pltpu.VMEM((4, 80, 384), BF),
             pltpu.VMEM((4, 80, 384), BF),
-            pltpu.VMEM((80, 384), F32),
-            pltpu.VMEM((2, 4, 80, 384), BF),
+            pltpu.VMEM((4, 80, 384), BF),
+            pltpu.VMEM((4, 80, 384), BF),
+            pltpu.VMEM((2, 80, 768), BF),
+            pltpu.VMEM((24, 128), F32),
+            pltpu.VMEM((2, 640, GROUP), F32),
+            pltpu.VMEM((2, 640, GROUP), BF),
             pltpu.VMEM((160, 6 * GROUP), F32),
             pltpu.SemaphoreType.DMA((N_COPIES,)),
             pltpu.SemaphoreType.DMA((N_COPIES,)),

time: 101 us -> 98.8 us (0.978)
  Pallas kernels: 97 us -> 95.6 us
    pallas_call x1, Pallas kernels: 97 us -> 95.6 us  [layer_call(): pl.pallas_call(layer_kernel, out_shape=jax.ShapeDtypeStruct((TOK, D), BF)...]
where the time goes in v5:
time: 98.8 us; the launch traced here: 98.6 us
  Pallas kernels  95.6 us (97%)
  other arithmetic  2.33 us (2%)
    pallas_call x1, Pallas kernels, layer_call(): pl.pallas_call(layer_kernel, out_shape=jax.ShapeDtypeStruct((TOK, D), BF)...  95.6 us

profile of v5, /device:TPU:1, one launch (start us, length us, event | category | flops | bytes accessed | tf_op | source)
XLA Modules:
  0.0 98.6 jit_solution(6322670548636796976)
XLA Ops:
  0.0 0.0 copy-start
  0.8 0.6 fusion.cond_ref
  1.4 95.6 %layer.1 = bf16[40,3072]{1,0:T(8,128)(2,1)} custom-call(bf16[40,3072]{1,0:T(8,128)(2,1)} %bitcast.14, bf16[1,512]{1,0:T(2,128)(2,1)} %fusion.cond_ref, bf16[576,512]{1,0:T(8,128)(2,1)} %bitcast.13, bf16[3,16,192,128]{3,2,1,0:T(8,128)(2,1)} %bitcast.12, bf16[128,3072]{1,0:T(8,128)(2,1)} %wo_hbm.1, f32[1,64]{1,0:T(1,128)} %bitcast.17, f32[1,64]{1,0:T(1,128)} %bitcast.18), custom_call_target="tpu_custom_call" | custom-call | tf_op jit(solution)/shard_map/layer/pallas_call | solution.py:554
  97.0 0.0 copy-done
  97.0 1.7 %select_bitcast_fusion = bf16[1,40,3072]{2,1,0:T(8,128)(2,1)} fusion(bf16[40,3072]{1,0:T(8,128)(2,1)S(1)} %copy-done, bf16[40,3072]{1,0:T(8,128)(2,1)} %layer.1, pred[]{:T(512)S(6)} %eq.3), kind=kLoop, calls=%fused_computation | loop fusion | flops 122880 | bytes 737281 | tf_op jit(solution)/shard_map/broadcast_in_dim | solution.py:603
  (1 shorter events, 0.0 us)
Async XLA Ops:
  0.0 97.0 %copy-start = (bf16[40,3072]{1,0:T(8,128)(2,1)S(1)}, bf16[40,3072]{1,0:T(8,128)(2,1)}, u32[]{:S(2)}) copy-start(bf16[40,3072]{1,0:T(8,128)(2,1)} %param.10) | copy-start | bytes 737284

commit v6 on v5

--- a/solution.py
+++ b/solution.py
@@ -115,7 +115,7 @@
     return c * lax.rsqrt(jnp.where(first, va, vb) + 1e-06) * gain
 
 
-N_COPIES = 176
+N_COPIES = 200
 
 
 def layer_kernel(
@@ -159,58 +159,70 @@
     top[...] = jnp.full(top.shape, -1e30, F32)
     ready()
 
-    link.send("w", lambda: w_hbm.at[:, f], lambda: wp.at[:, f], here.yhi)
-
-    def send_tok(j):
+    for g in range(2):
+        src = lambda g=g: w_hbm.at[:, f, pl.ds(96 * g, 96)]
+        link.send(("w", g, "y"), src, lambda g=g: wp.at[:, f, pl.ds(96 * g, 96)], here.yhi)
+
+    def send_tok(j, h):
         src = (0, 1, 3)[j], (0, 2, 4)[j]
         dst = (1, 3, 5)[j], (2, 4, 6)[j]
-        link.send(("up", j), lambda: blocks.at[src[0]], lambda: blocks.at[dst[0]], here.zp)
-        link.send(("down", j), lambda: blocks.at[src[1]], lambda: blocks.at[dst[1]], here.zm)
-
-    def wait_tok(j):
+        link.send(("up", j, h), lambda: blocks.at[src[0], h], lambda: blocks.at[dst[0], h], here.zp)
+        link.send(("down", j, h), lambda: blocks.at[src[1], h], lambda: blocks.at[dst[1], h], here.zm)
+
+    def wait_tok(j, h):
         dst = (1, 3, 5)[j], (2, 4, 6)[j]
-        link.wait(("up", j), lambda: blocks.at[dst[0]], here.zm)
-        link.wait(("down", j), lambda: blocks.at[dst[1]], here.zp)
-
-    send_tok(0)
+        link.wait(("up", j, h), lambda: blocks.at[dst[0], h], here.zm)
+        link.wait(("down", j, h), lambda: blocks.at[dst[1], h], here.zp)
+
+    send_tok(0, 0)
+    send_tok(0, 1)
     for d, dev in enumerate(seq_peers):
         link.send(("mod", d + 1), lambda: modbuf.at[s], lambda: modbuf.at[s], dev)
 
-    def slice_of(who, half=None):
+    def slice_of(who, g, half=None):
         if half is None:
-            return lambda: wp.at[:, who]
-        return lambda: wp.at[:, who, pl.ds(96 * half, 96)]
-
-    def w_send(name, who, dev, half=None):
-        link.send(("w", name), slice_of(who, half), slice_of(who, half), dev)
-
-    def w_wait(name, who, half=None):
-        link.wait(("w", name), slice_of(who, half), here.sib)
-
-    def w_spread(y):
+            return lambda: wp.at[:, who, pl.ds(96 * g, 96)]
+        return lambda: wp.at[:, who, pl.ds(96 * g + 48 * half, 48)]
+
+    def w_send(name, who, g, dev, half=None):
+        link.send(("w", g, name), slice_of(who, g, half), slice_of(who, g, half), dev)
+
+    def w_wait(name, who, g, half=None):
+        link.wait(("w", g, name), slice_of(who, g, half), here.sib)
+
+    def w_spread(y, g):
         who = here.frame_at(y, 0, 0)
-        w_send((y, "xp"), who, here.xp)
-        w_send((y, "xm"), who, here.xm)
-        w_send((y, "s0"), who, here.sib)
-
-    def w_relay(y):
+        w_send((y, "xp"), who, g, here.xp)
+        w_send((y, "xm"), who, g, here.xm)
+        w_send((y, "s0"), who, g, here.sib)
+
+    def w_begin(g):
+        w_wait("y", f, g)
+        w_send("ylo", f, g, here.ylo)
+        w_spread(0, g)
+
+    def w_second(g):
+        w_wait("ylo", here.frame_at(1, 0, 0), g)
+        w_spread(1, g)
+
+    def w_relay(y, g):
         left, right = here.frame_at(y, 3, 0), here.frame_at(y, 1, 0)
-        w_wait((y, "xp"), left)
-        w_send((y, "xp2"), left, here.xp, 0)
-        w_send((y, "s3"), left, here.sib)
-        w_wait((y, "xm"), right)
-        w_send((y, "xm2"), right, here.xm, 1)
-        w_send((y, "s1"), right, here.sib)
-
-    def w_finish(y):
+        w_wait((y, "xp"), left, g)
+        w_send((y, "xp2"), left, g, here.xp, 0)
+        w_send((y, "s3"), left, g, here.sib)
+        w_wait((y, "xm"), right, g)
+        w_send((y, "xm2"), right, g, here.xm, 1)
+        w_send((y, "s1"), right, g, here.sib)
+
+    def w_finish(y, g):
         far = here.frame_at(y, 2, 0)
-        w_wait((y, "xp2"), far, 0)
-        w_wait((y, "xm2"), far, 1)
-        w_send((y, "s2"), far, here.sib)
-
-    def w_from_sib(y):
+        w_wait((y, "xp2"), far, g, 0)
+        w_wait((y, "xm2"), far, g, 1)
+        w_send((y, "s2"), far, g, here.sib)
+
+    def w_from_sib(y, g):
         for dx in range(4):
-            w_wait((y, f"s{dx}"), here.frame_at(y, dx, 1))
+            w_wait((y, f"s{dx}"), here.frame_at(y, dx, 1), g)
 
     def wo_at(zz, c, h):
         return lambda: wz.at[zz, c, h]
@@ -371,16 +383,19 @@
             kv_wait(p, (3, y), 1)
         to_sib(p, 3)
 
-    w_wait0 = lambda: wp.at[:, f]
-    link.wait("w", w_wait0, here.yhi)
-    w_send("ylo", f, here.ylo)
-    w_spread(0)
-
-    wait_tok(0)
-    send_tok(1)
-    w_wait("ylo", here.frame_at(1, 0, 0))
-    w_spread(1)
-    w_relay(0)
+    w_begin(0)
+    w_begin(1)
+    wait_tok(0, 0)
+    send_tok(1, 0)
+    w_second(0)
+    w_relay(0, 0)
+    wait_tok(0, 1)
+    send_tok(1, 1)
+    w_second(1)
+    w_relay(0, 1)
+    wait_tok(1, 0)
+    send_tok(2, 0)
+    w_relay(1, 0)
     for d in range(1, 16):
         peer = lax.rem(s + 16 - d, 16)
         link.wait(("mod", d), lambda: modbuf.at[peer], (f, peer))
@@ -390,31 +405,34 @@
         modt[9 * i + 4 : 9 * i + 5, :] = low[4:5] + high[0:1]
         modt[9 * i + 5 : 9 * i + 9, :] = high[1:5]
     modulate(1, 1, 2)
-    w_finish(0)
+    wait_tok(1, 1)
+    send_tok(2, 1)
+    w_relay(1, 1)
+    for g in range(2):
+        w_finish(0, g)
+    modulate(2, 3, 4)
+    wait_tok(2, 0)
+    link.send(("up", 3), lambda: blocks.at[5, 0], lambda: blocks.at[7, 0], here.zp)
     local[1].wait()
-
-    wait_tok(1)
-    send_tok(2)
-    w_relay(1)
-    modulate(2, 3, 4)
-    w_finish(1)
-    w_from_sib(0)
-    w_from_sib(1)
+    for g in range(2):
+        w_finish(1, g)
+    for g in range(2):
+        w_from_sib(0, g)
+        w_from_sib(1, g)
     project(1, 2)
 
-    wait_tok(2)
-    link.send(("up", 3), lambda: blocks.at[5, 0], lambda: blocks.at[7, 0], here.zp)
+    wait_tok(2, 1)
     link.send(("down", 3), lambda: blocks.at[6, 1], lambda: blocks.at[7, 1], here.zm)
+    modulate(3, 5, 6)
+    project(3)
     begin(1)
     begin(2)
-    modulate(3, 5, 6)
-    project(3)
     link.wait(("up", 3), lambda: blocks.at[7, 0], here.zm)
     link.wait(("down", 3), lambda: blocks.at[7, 1], here.zp)
     wo_start()
-    arrive_y(1)
     modulate(0, 0, 7)
     project(0)
+    arrive_y(1)
     begin(3)
     for p in (1, 2, 3, 0):
         link.wait(("qswap", p), lambda p=p: qin.at[p], here.yhi)
@@ -496,8 +514,8 @@
 
     lax.fori_loop(0, 16, step, 0)
 
-    upper_part = acc[0:64, 0:640] / acc[64:65, 0:640]
-    lower_part = acc[64:128, 640:1280] / acc[0:1, 640:1280]
+    upper_part = acc[0:64, 0:640] * (1.0 / acc[64:65, 0:640])
+    lower_part = acc[64:128, 640:1280] * (1.0 / acc[0:1, 640:1280])
     mixed[...] = jnp.concatenate([upper_part, lower_part], axis=0).T
 
     def rows_of(p, b):

time: 98.8 us -> 97.8 us (0.990)
  Pallas kernels: 95.6 us -> 94.6 us
where the time goes in v6:
time: 97.8 us; the launch traced here: 97.7 us
  Pallas kernels  94.6 us (97%)
  other arithmetic  2.33 us (2%)
    pallas_call x1, Pallas kernels, layer_call(): pl.pallas_call(layer_kernel, out_shape=jax.ShapeDtypeStruct((TOK, D), BF)...  94.6 us

profile of v6, /device:TPU:1, one launch (start us, length us, event | category | flops | bytes accessed | tf_op | source)
XLA Modules:
  0.0 97.7 jit_solution(10574251390040178784)
XLA Ops:
  0.0 0.0 copy-start
  0.8 0.6 fusion.cond_ref
  1.4 94.6 %layer.1 = bf16[40,3072]{1,0:T(8,128)(2,1)} custom-call(bf16[40,3072]{1,0:T(8,128)(2,1)} %bitcast.14, bf16[1,512]{1,0:T(2,128)(2,1)} %fusion.cond_ref, bf16[576,512]{1,0:T(8,128)(2,1)} %bitcast.13, bf16[3,16,192,128]{3,2,1,0:T(8,128)(2,1)} %bitcast.12, bf16[128,3072]{1,0:T(8,128)(2,1)} %wo_hbm.1, f32[1,64]{1,0:T(1,128)} %bitcast.17, f32[1,64]{1,0:T(1,128)} %bitcast.18), custom_call_target="tpu_custom_call" | custom-call | tf_op jit(solution)/shard_map/layer/pallas_call | solution.py:572
  96.0 0.0 copy-done
  96.0 1.7 %select_bitcast_fusion = bf16[1,40,3072]{2,1,0:T(8,128)(2,1)} fusion(bf16[40,3072]{1,0:T(8,128)(2,1)S(1)} %copy-done, bf16[40,3072]{1,0:T(8,128)(2,1)} %layer.1, pred[]{:T(512)S(6)} %eq.3), kind=kLoop, calls=%fused_computation | loop fusion | flops 122880 | bytes 737281 | tf_op jit(solution)/shard_map/broadcast_in_dim | solution.py:621
  (1 shorter events, 0.0 us)
Async XLA Ops:
  0.0 96.0 %copy-start = (bf16[40,3072]{1,0:T(8,128)(2,1)S(1)}, bf16[40,3072]{1,0:T(8,128)(2,1)}, u32[]{:S(2)}) copy-start(bf16[40,3072]{1,0:T(8,128)(2,1)} %param.10) | copy-start | bytes 737284

commit v7 on v6

--- a/solution.py
+++ b/solution.py
@@ -242,13 +242,18 @@
             link.wait(("wo", way, d, h), at, dev)
             if d < 3 or (d == 3 and h == last):
                 link.send(("wo", way, d + 1, h), at, at, dev)
-            link.send(("wo", "sib", way, d, h), at, at, here.sib)
+            if d == 4:
+                link.send(("wo", "sib", way, d), at, at, here.sib)
+            elif h == 1:
+                whole = lambda zz=zz: wz.at[zz, core]
+                link.send(("wo", "sib", way, d), whole, whole, here.sib)
 
     def wo_from_sib(d, h):
         for way, zz, last in (("up", here.z_at(-d), 0), ("down", here.z_at(d), 1)):
-            if d == 4 and h != last:
-                continue
-            link.wait(("wo", "sib", way, d, h), wo_at(zz, 1 - core, h), here.sib)
+            if d == 4 and h == last:
+                link.wait(("wo", "sib", way, d), wo_at(zz, 1 - core, h), here.sib)
+            if d < 4 and h == 1:
+                link.wait(("wo", "sib", way, d), lambda zz=zz: wz.at[zz, 1 - core], here.sib)
 
     first = lax.broadcasted_iota(jnp.int32, (1, GROUP), 1) < HEAD
     q_scale = math.log2(math.e) / math.sqrt(HEAD)

time: 97.8 us -> 98.2 us (level)
  no operation moved by 1% of the time
where the time goes in v7:
time: 98.2 us; the launch traced here: 98 us
  Pallas kernels  95 us (97%)
  other arithmetic  2.33 us (2%)
    pallas_call x1, Pallas kernels, layer_call(): pl.pallas_call(layer_kernel, out_shape=jax.ShapeDtypeStruct((TOK, D), BF)...  95 us

profile of v7, /device:TPU:1, one launch (start us, length us, event | category | flops | bytes accessed | tf_op | source)
XLA Modules:
  0.0 98.0 jit_solution(14252625677853573427)
XLA Ops:
  0.0 0.0 copy-start
  0.8 0.6 fusion.cond_ref
  1.4 95.0 %layer.1 = bf16[40,3072]{1,0:T(8,128)(2,1)} custom-call(bf16[40,3072]{1,0:T(8,128)(2,1)} %bitcast.14, bf16[1,512]{1,0:T(2,128)(2,1)} %fusion.cond_ref, bf16[576,512]{1,0:T(8,128)(2,1)} %bitcast.13, bf16[3,16,192,128]{3,2,1,0:T(8,128)(2,1)} %bitcast.12, bf16[128,3072]{1,0:T(8,128)(2,1)} %wo_hbm.1, f32[1,64]{1,0:T(1,128)} %bitcast.17, f32[1,64]{1,0:T(1,128)} %bitcast.18), custom_call_target="tpu_custom_call" | custom-call | tf_op jit(solution)/shard_map/layer/pallas_call | solution.py:577
  96.4 0.0 copy-done
  96.4 1.7 %select_bitcast_fusion = bf16[1,40,3072]{2,1,0:T(8,128)(2,1)} fusion(bf16[40,3072]{1,0:T(8,128)(2,1)S(1)} %copy-done, bf16[40,3072]{1,0:T(8,128)(2,1)} %layer.1, pred[]{:T(512)S(6)} %eq.3), kind=kLoop, calls=%fused_computation | loop fusion | flops 122880 | bytes 737281 | tf_op jit(solution)/shard_map/broadcast_in_dim | solution.py:626
  (1 shorter events, 0.0 us)
Async XLA Ops:
  0.0 96.4 %copy-start = (bf16[40,3072]{1,0:T(8,128)(2,1)S(1)}, bf16[40,3072]{1,0:T(8,128)(2,1)}, u32[]{:S(2)}) copy-start(bf16[40,3072]{1,0:T(8,128)(2,1)} %param.10) | copy-start | bytes 737284
